TPU v7x, 32 devices: a whole 2x2x4 slice. The times are simulated.
32 devices in a mesh: dp: 8 (over y, x, core), head: 4 (over z).
Axes of the slice: x: 2, y: 2, z: 4, core: 2. Of those that a mesh axis runs over, the one named last changes fastest.
Arguments:
- tokens: bfloat16 [12288, 768], P(('dp', 'head')), may hold values from -6 to 6
- lengths: int32 [8, 4], P('dp'), may hold values from 1 to 1533, as said below
- ln1_gain: float32 [768], replicated, may hold values from 0.5 to 1.5
- ln1_bias: float32 [768], replicated, may hold values from -3 to 3
- w_qkv: bfloat16 [768, 2304], replicated, may hold values from -0.21875 to 0.21875
- bias_q: float32 [768], replicated, may hold values from -3 to 3
- bias_v: float32 [768], replicated, may hold values from -3 to 3
- w_out: bfloat16 [768, 768], replicated, may hold values from -3.5 to 3.5
- bias_out: float32 [768], replicated, may hold values from -3 to 3
- ln2_gain: float32 [768], replicated, may hold values from 0.5 to 1.5
- ln2_bias: float32 [768], replicated, may hold values from -3 to 3
- w_fc: bfloat16 [768, 3072], replicated, may hold values from -0.21875 to 0.21875
- bias_fc: float32 [3072], replicated, may hold values from -3 to 3
- w_proj: bfloat16 [3072, 768], replicated, may hold values from -0.625 to 0.625
- bias_proj: float32 [768], replicated, may hold values from -3 to 3
- cotangent: bfloat16 [12288, 768], P(('dp', 'head')), may hold values from -6 to 6
Outputs:
- block_output: float32 [12288, 768], P(('dp', 'head'))
- grad_tokens: float32 [12288, 768], P(('dp', 'head'))
- grad_ln1_gain: float32 [768], replicated
- grad_ln1_bias: float32 [768], replicated
- grad_w_qkv: float32 [768, 2304], P('dp')
- grad_bias_q: float32 [768], replicated
- grad_bias_v: float32 [768], replicated
- grad_w_out: float32 [768, 768], P('dp')
- grad_bias_out: float32 [768], replicated
- grad_ln2_gain: float32 [768], replicated
- grad_ln2_bias: float32 [768], replicated
- grad_w_fc: float32 [768, 3072], P(None, 'dp')
- grad_bias_fc: float32 [3072], replicated
- grad_w_proj: float32 [3072, 768], P('dp')
- grad_bias_proj: float32 [768], replicated
Inputs may be any that keep to these rules, and one draw needn't show every extreme that they name: Each row of lengths adds up to 1536; one sequence of each row holds at least 1248 tokens.
All inputs are finite; a program needn't handle non-finite values.
Results may differ from a plain program's by a relative error of at most 0.012.
Values may be sent and summed in bfloat16 or wider, within the bound.
A program may use at most 192 MiB of HBM per device.

v0:
```python
import math

import jax
import jax.numpy as jnp
from jax import lax
from jax.sharding import PartitionSpec as P

HEAD_DIM = 64


EPSILON = 1e-05
DEPTH_SCALE = 1.0 / math.sqrt(12.0)


def layer_norm(values, gain_vec, bias_vec):
    center = jnp.mean(values, axis=-1, keepdims=True)
    centered = values - center
    spread = jnp.mean(centered * centered, axis=-1, keepdims=True)
    return centered * lax.rsqrt(spread + EPSILON) * gain_vec + bias_vec


def contract_rows(left_matrix, right_matrix):
    return lax.dot_general(
        left_matrix, right_matrix, (((0,), (0,)), ((), ())), preferred_element_type=jnp.float32
    )


def contract_cols(left_matrix, right_matrix):
    return lax.dot_general(
        left_matrix, right_matrix, (((1,), (1,)), ((), ())), preferred_element_type=jnp.float32
    )


def sequence_ids(counts, group_tok):
    seq_ends = jnp.cumsum(counts)
    places = jnp.arange(group_tok, dtype=jnp.int32)
    return jnp.sum((places[:, None] >= seq_ends[None, :]).astype(jnp.int32), axis=1)


def block_weights(query_block, key_heads, seq_ids, offset):
    group_tok = key_heads.shape[0]
    block_size = query_block.shape[0]
    places = jnp.arange(group_tok, dtype=jnp.int32)
    rows_here = offset + jnp.arange(block_size, dtype=jnp.int32)
    block_ids = lax.dynamic_slice_in_dim(seq_ids, offset, block_size, 0)
    allowed = (places[None, :] <= rows_here[:, None]) & (seq_ids[None, :] == block_ids[:, None])
    raw_scores = jnp.einsum(
        "qhd,khd->hqk", query_block, key_heads, preferred_element_type=jnp.float32
    )
    scores = jnp.where(allowed[None], raw_scores * HEAD_DIM ** (-0.5), -1e30)
    largest = jnp.max(scores, axis=-1, keepdims=True)
    weights = jnp.exp(scores - largest)
    return weights / jnp.sum(weights, axis=-1, keepdims=True)


def split_heads(group_mixed):
    group_tok, _three, part_width = group_mixed.shape
    head_count = part_width // HEAD_DIM
    shaped = group_mixed.reshape(group_tok, 3, head_count, HEAD_DIM)
    return (shaped[:, 0], shaped[:, 1], shaped[:, 2])


def attention_forward(group_mixed, seq_ids):
    group_tok = group_mixed.shape[0]
    part_width = group_mixed.shape[2]
    query_heads, key_heads, value_heads = split_heads(group_mixed)
    block_size = min(512, group_tok)

    def one_block(block_index):
        offset = block_index * block_size
        query_block = lax.dynamic_slice_in_dim(query_heads, offset, block_size, 0)
        soft_weights = block_weights(query_block, key_heads, seq_ids, offset)
        return jnp.einsum(
            "hqk,khd->qhd",
            soft_weights.astype(jnp.bfloat16),
            value_heads,
            preferred_element_type=jnp.float32,
        )

    blocks = lax.map(one_block, jnp.arange(group_tok // block_size, dtype=jnp.int32))
    return blocks.reshape(group_tok, part_width)


def attention_backward(group_mixed, group_grad, seq_ids):
    group_tok = group_mixed.shape[0]
    part_width = group_mixed.shape[2]
    query_heads, key_heads, value_heads = split_heads(group_mixed)
    grad_heads = group_grad.reshape(group_tok, part_width // HEAD_DIM, HEAD_DIM)
    block_size = min(512, group_tok)

    def one_block(running, block_index):
        key_grad, value_grad = running
        offset = block_index * block_size
        query_block = lax.dynamic_slice_in_dim(query_heads, offset, block_size, 0)
        grad_block = lax.dynamic_slice_in_dim(grad_heads, offset, block_size, 0)
        soft_weights = block_weights(query_block, key_heads, seq_ids, offset)
        weight_grad = jnp.einsum(
            "qhd,khd->hqk", grad_block, value_heads, preferred_element_type=jnp.float32
        )
        centre = jnp.sum(soft_weights * weight_grad, axis=-1, keepdims=True)
        score_grad = (soft_weights * (weight_grad - centre) * HEAD_DIM ** (-0.5)).astype(
            jnp.bfloat16
        )
        value_grad = value_grad + jnp.einsum(
            "hqk,qhd->khd",
            soft_weights.astype(jnp.bfloat16),
            grad_block,
            preferred_element_type=jnp.float32,
        )
        key_grad = key_grad + jnp.einsum(
            "hqk,qhd->khd", score_grad, query_block, preferred_element_type=jnp.float32
        )
        query_grad = jnp.einsum(
            "hqk,khd->qhd", score_grad, key_heads, preferred_element_type=jnp.float32
        )
        return ((key_grad, value_grad), query_grad)

    empty_grad = jnp.zeros(key_heads.shape, jnp.float32)
    (key_grad, value_grad), query_blocks = lax.scan(
        one_block, (empty_grad, empty_grad), jnp.arange(group_tok // block_size, dtype=jnp.int32)
    )
    query_grad = query_blocks.reshape(group_tok, part_width)
    stacked = jnp.stack(
        [
            query_grad,
            key_grad.reshape(group_tok, part_width),
            value_grad.reshape(group_tok, part_width),
        ],
        axis=1,
    )
    return stacked.astype(jnp.bfloat16)


def forward(source_rows, seq_ids, weight_set):
    (
        ln1_gain,
        ln1_bias,
        w_qkv,
        bias_q,
        bias_v,
        w_out,
        bias_out,
        ln2_gain,
        ln2_bias,
        w_fc,
        bias_fc,
        w_proj,
        bias_proj,
    ) = weight_set
    tok_rows, model_width = source_rows.shape
    source = source_rows.astype(jnp.float32)
    normed = layer_norm(source, ln1_gain, ln1_bias).astype(jnp.bfloat16)
    offsets = jnp.concatenate([bias_q, jnp.zeros_like(bias_q), bias_v])
    mixed_rows = (jnp.dot(normed, w_qkv, preferred_element_type=jnp.float32) + offsets).astype(
        jnp.bfloat16
    )
    group_mixed = lax.all_to_all(
        mixed_rows.reshape(tok_rows, 3, model_width),
        "head",
        split_axis=2,
        concat_axis=0,
        tiled=True,
    )
    attended = attention_forward(group_mixed, seq_ids).astype(jnp.bfloat16)
    back_rows = lax.all_to_all(attended, "head", split_axis=0, concat_axis=1, tiled=True)
    middle = source + DEPTH_SCALE * (
        jnp.dot(back_rows, w_out, preferred_element_type=jnp.float32) + bias_out
    )
    second = layer_norm(middle, ln2_gain, ln2_bias).astype(jnp.bfloat16)
    pre_act = jnp.dot(second, w_fc, preferred_element_type=jnp.float32) + bias_fc
    hidden = jax.nn.gelu(pre_act, approximate=True).astype(jnp.bfloat16)
    result = middle + DEPTH_SCALE * (
        jnp.dot(hidden, w_proj, preferred_element_type=jnp.float32) + bias_proj
    )
    return (source, normed, group_mixed, back_rows, middle, second, pre_act, hidden, result)


def gelu_tanh(inputs_pre):
    return jax.nn.gelu(inputs_pre, approximate=True)


def shards(
    tokens,
    lengths,
    ln1_gain,
    ln1_bias,
    w_qkv,
    bias_q,
    bias_v,
    w_out,
    bias_out,
    ln2_gain,
    ln2_bias,
    w_fc,
    bias_fc,
    w_proj,
    bias_proj,
    cotangent,
):
    tok_rows, model_width = tokens.shape
    group_tok = tok_rows * lax.axis_size("head")
    device_count = lax.axis_size("dp") * lax.axis_size("head")
    grad_scale = 1.0 / math.sqrt(tok_rows * device_count)
    seq_ids = sequence_ids(lengths[0], group_tok)
    weight_set = (
        ln1_gain,
        ln1_bias,
        w_qkv,
        bias_q,
        bias_v,
        w_out,
        bias_out,
        ln2_gain,
        ln2_bias,
        w_fc,
        bias_fc,
        w_proj,
        bias_proj,
    )
    kept = forward(tokens, seq_ids, weight_set)
    block_output = kept[8]
    fresh_tokens, fresh_weights, fresh_grad = lax.optimization_barrier(
        (tokens, weight_set, cotangent)
    )
    kept = forward(fresh_tokens, seq_ids, fresh_weights)
    grad_rows = fresh_grad.astype(jnp.float32)
    source, normed, group_mixed, back_rows, middle, second, pre_act, hidden, result = kept
    grad_bias_proj = DEPTH_SCALE * jnp.sum(grad_rows, axis=0)
    proj_grad = (DEPTH_SCALE * grad_rows).astype(jnp.bfloat16)
    grad_w_proj = contract_rows(hidden, proj_grad)
    hidden_grad = contract_cols(proj_grad, w_proj)
    gelu_value, gelu_pull = jax.vjp(gelu_tanh, pre_act)
    (pre_grad,) = gelu_pull(hidden_grad)
    grad_bias_fc = jnp.sum(pre_grad, axis=0)
    fc_grad = pre_grad.astype(jnp.bfloat16)
    grad_w_fc = contract_rows(second, fc_grad)
    second_grad = contract_cols(fc_grad, w_fc)
    norm_value, second_pull = jax.vjp(layer_norm, middle, ln2_gain, ln2_bias)
    middle_part, grad_ln2_gain, grad_ln2_bias = second_pull(second_grad)
    middle_grad = grad_rows + middle_part
    grad_bias_out = DEPTH_SCALE * jnp.sum(middle_grad, axis=0)
    out_grad = (DEPTH_SCALE * middle_grad).astype(jnp.bfloat16)
    grad_w_out = contract_rows(back_rows, out_grad)
    attended_grad = contract_cols(out_grad, w_out).astype(jnp.bfloat16)
    group_grad = lax.all_to_all(attended_grad, "head", split_axis=1, concat_axis=0, tiled=True)
    group_mixed_grad = attention_backward(group_mixed, group_grad, seq_ids)
    mixed_grad = lax.all_to_all(
        group_mixed_grad, "head", split_axis=0, concat_axis=2, tiled=True
    ).reshape(tok_rows, 3 * model_width)
    grad_w_qkv = contract_rows(normed, mixed_grad)
    grad_bias_q = jnp.sum(mixed_grad[:, :model_width], axis=0, dtype=jnp.float32)
    grad_bias_v = jnp.sum(mixed_grad[:, 2 * model_width :], axis=0, dtype=jnp.float32)
    normed_grad = contract_cols(mixed_grad, w_qkv)
    first_value, first_pull = jax.vjp(layer_norm, source, ln1_gain, ln1_bias)
    token_part, grad_ln1_gain, grad_ln1_bias = first_pull(normed_grad)
    grad_tokens = middle_grad + token_part
    mat_shares = (
        lax.psum_scatter(grad_w_qkv * grad_scale, "dp", scatter_dimension=0, tiled=True),
        lax.psum_scatter(grad_w_out * grad_scale, "dp", scatter_dimension=0, tiled=True),
        lax.psum_scatter(grad_w_fc * grad_scale, "dp", scatter_dimension=1, tiled=True),
        lax.psum_scatter(grad_w_proj * grad_scale, "dp", scatter_dimension=0, tiled=True),
    )
    qkv_total, out_total, fc_total, proj_total = (
        lax.psum(mat_shares[0].astype(jnp.bfloat16), "head").astype(jnp.float32),
        lax.psum(mat_shares[1].astype(jnp.bfloat16), "head").astype(jnp.float32),
        lax.psum(mat_shares[2].astype(jnp.bfloat16), "head").astype(jnp.float32),
        lax.psum(mat_shares[3].astype(jnp.bfloat16), "head").astype(jnp.float32),
    )
    vec_totals = lax.psum(
        (
            grad_ln1_gain * grad_scale,
            grad_ln1_bias * grad_scale,
            grad_bias_q * grad_scale,
            grad_bias_v * grad_scale,
            grad_bias_out * grad_scale,
            grad_ln2_gain * grad_scale,
            grad_ln2_bias * grad_scale,
            grad_bias_fc * grad_scale,
            grad_bias_proj * grad_scale,
        ),
        ("dp", "head"),
    )
    ln1g_total, ln1b_total, bq_total, bv_total, bout_total = (
        vec_totals[0],
        vec_totals[1],
        vec_totals[2],
        vec_totals[3],
        vec_totals[4],
    )
    ln2g_total, ln2b_total, bfc_total, bproj_total = (
        vec_totals[5],
        vec_totals[6],
        vec_totals[7],
        vec_totals[8],
    )
    return (
        block_output,
        grad_tokens,
        ln1g_total,
        ln1b_total,
        qkv_total,
        bq_total,
        bv_total,
        out_total,
        bout_total,
        ln2g_total,
        ln2b_total,
        fc_total,
        bfc_total,
        proj_total,
        bproj_total,
    )


def solution(mesh):
    return jax.shard_map(
        shards,
        mesh=mesh,
        in_specs=(
            P(("dp", "head"), None),
            P("dp", None),
            P(),
            P(),
            P(),
            P(),
            P(),
            P(),
            P(),
            P(),
            P(),
            P(),
            P(),
            P(),
            P(),
            P(("dp", "head"), None),
        ),
        out_specs=(
            P(("dp", "head"), None),
            P(("dp", "head"), None),
            P(),
            P(),
            P("dp", None),
            P(),
            P(),
            P("dp", None),
            P(),
            P(),
            P(),
            P(None, "dp"),
            P(),
            P("dp", None),
            P(),
        ),
        check_vma=False,
    )
```

profile of v0, /device:TPU:0, one launch (start us, length us, event | category | flops | bytes accessed | tf_op | source)
XLA Modules:
  0.0 922.4 jit_solution(10704001914628803205)
XLA Ops:
  24.2 6.4 all-to-all-start.2
  31.1 53.5 %all-to-all-done.2 = bf16[384,3,768]{0,1,2:T(4,128)(2,1)} async-done(((bf16[384,3,768]{0,1,2:T(4,128)(2,1)}), bf16[384,3,768]{0,1,2:T(4,128)(2,1)}, u32[]{:S(2)}, u32[]{:S(2)}) %all-to-all-start.2) | async-done | bytes 1769504 | tf_op jit(solution)/shard_map/all_to_all | solution.py:157
  96.6 85.8 %while.36 = (s32[]{:T(128)}, bf16[3,512,3,64]{1,3,2,0:T(8,128)(2,1)}, s32[3]{0:T(128)S(1)}, s32[1536]{0:T(1024)S(1)}, bf16[1536,3,64]{0,2,1:T(8,128)(2,1)}, /*in...) while((s32[]{:T(128)}, ...), condition=%wide.region_15.16_spmd, body=%wide.region_12.15_spmd.sunk | while | flops 625215488 | bytes 43479760 | solution.py:80
  104.9 14.3 %fusion.239 = (f32[3,512]{1,0:T(4,128)S(1)}, f32[3,512,1536]{2,1,0:T(8,128)}) fusion(f32[3,512,1536]{2,1,0:T(8,128)} %fusion.237, pred[512,1536]{1,0:T(8,128)(4,1)S(1)} %fusion.238), kind=kOutput, calls=%fused_computation.222.clone.1 | output fusion | flops 14157311 | bytes 19666944 | tf_op jit(solution)/shard_map/while/body/eval_jaxpr/sub | solution.py:52
  133.5 14.3 %fusion.239 = (f32[3,512]{1,0:T(4,128)S(1)}, f32[3,512,1536]{2,1,0:T(8,128)}) fusion(f32[3,512,1536]{2,1,0:T(8,128)} %fusion.237, pred[512,1536]{1,0:T(8,128)(4,1)S(1)} %fusion.238), kind=kOutput, calls=%fused_computation.222.clone.1 | output fusion | flops 14157311 | bytes 19666944 | tf_op jit(solution)/shard_map/while/body/eval_jaxpr/sub | solution.py:52
  162.1 14.3 %fusion.239 = (f32[3,512]{1,0:T(4,128)S(1)}, f32[3,512,1536]{2,1,0:T(8,128)}) fusion(f32[3,512,1536]{2,1,0:T(8,128)} %fusion.237, pred[512,1536]{1,0:T(8,128)(4,1)S(1)} %fusion.238), kind=kOutput, calls=%fused_computation.222.clone.1 | output fusion | flops 14157311 | bytes 19666944 | tf_op jit(solution)/shard_map/while/body/eval_jaxpr/sub | solution.py:52
  188.9 18.0 %all_to_all.93 = bf16[4,384,192]{1,2,0:T(8,128)(2,1)S(1)} all-to-all(bf16[4,384,192]{1,2,0:T(8,128)(2,1)S(1)} %copy.100), channel_id=1, replica_groups=mesh['dp'=8,'head'=4] {'head'}, dimensions={0} | all-to-all | bytes 1179648 | tf_op jit(solution)/shard_map/all_to_all | solution.py:165
  235.6 8.7 convolution_multiply_fusion.2
  256.3 236.1 %while.37 = (s32[]{:T(128)}, f32[1536,3,64]{0,2,1:T(8,128)}, f32[1536,3,64]{0,2,1:T(8,128)}, bf16[3,512,3,64]{1,3,2,0:T(8,128)(2,1)}, s32[3]{0:T(128)S(1)}, /*in...) while((s32[]{:T(128)}, f32[1536,3,64]{0,2,1:T(8,128)}, ...), condition=%wide.region_24.25_spmd.clone, body=%wide.region_20.24_spmd.clone.sunk | while | flops 1565401088 | bytes 134347520 | solution.py:119
  265.1 16.7 %fusion.254 = (f32[3,512]{1,0:T(4,128)}, f32[3,512,1536]{2,1,0:T(8,128)}) fusion(f32[3,512,1536]{2,1,0:T(8,128)} %fusion.252, pred[512,1536]{1,0:T(8,128)(4,1)S(1)} %fusion.253), kind=kOutput, calls=%fused_computation.223.clone.1 | output fusion | flops 14157311 | bytes 19666944 | tf_op jit(solution)/shard_map/while/body/eval_jaxpr/sub | solution.py:52
  281.8 7.0 fusion.251
  288.7 20.1 %fusion.257 = bf16[3,512,3,64]{1,3,2,0:T(8,128)(2,1)} fusion(bf16[3,512,3,64]{1,3,2,0:T(8,128)(2,1)} %get-tuple-element.556, s32[]{:T(128)} %get-tuple-element.553, bf16[1536,3,64]{0,2,1:T(8,128)(2,1)} %get-tuple-element.574, f32[3,512,1536]{2,1,0:T(8,128)} %fusion.251, f32[3,512,1536]{2,1,0:T(8,128)} %get-tuple-element.471, ...), kind=kOutput, calls=%fused_computation.61.clone.1 | convolution fusion | flops 318508032 | bytes 38748672 | tf_op jit(solution)/shard_map/while/body/eval_jaxpr/hqk,khd->qhd/dot_general | solution.py:113
  314.9 21.6 %fusion.255 = f32[1536,3,64]{0,2,1:T(8,128)} fusion(f32[3,512,1536]{2,1,0:T(8,128)} %fusion.251, f32[1536,3,64]{0,2,1:T(8,128)} %get-tuple-element.554, pred[]{:T(512)S(6)} %compare.3, bf16[1536,3,64]{0,2,1:T(8,128)(2,1)} %get-tuple-element.572, s32[]{:T(128)S(6)} %select_n.66, f32[3,512,1536]{2,1,0:T(8,128)} %get-tuple-element.471, ...), kind=kOutput, calls=%fused_computation.59.clone.1 | convolution fusion | flops 319097856 | bytes 40321028 | tf_op jit(solution)/shard_map/while/body/eval_jaxpr/hqk,qhd->khd/dot_general | solution.py:110
  344.9 15.3 %fusion.254 = (f32[3,512]{1,0:T(4,128)}, f32[3,512,1536]{2,1,0:T(8,128)}) fusion(f32[3,512,1536]{2,1,0:T(8,128)} %fusion.252, pred[512,1536]{1,0:T(8,128)(4,1)S(1)} %fusion.253), kind=kOutput, calls=%fused_computation.223.clone.1 | output fusion | flops 14157311 | bytes 19666944 | tf_op jit(solution)/shard_map/while/body/eval_jaxpr/sub | solution.py:52
  366.3 20.1 %fusion.257 = bf16[3,512,3,64]{1,3,2,0:T(8,128)(2,1)} fusion(bf16[3,512,3,64]{1,3,2,0:T(8,128)(2,1)} %get-tuple-element.556, s32[]{:T(128)} %get-tuple-element.553, bf16[1536,3,64]{0,2,1:T(8,128)(2,1)} %get-tuple-element.574, f32[3,512,1536]{2,1,0:T(8,128)} %fusion.251, f32[3,512,1536]{2,1,0:T(8,128)} %get-tuple-element.471, ...), kind=kOutput, calls=%fused_computation.61.clone.1 | convolution fusion | flops 318508032 | bytes 38748672 | tf_op jit(solution)/shard_map/while/body/eval_jaxpr/hqk,khd->qhd/dot_general | solution.py:113
  392.4 21.9 %fusion.255 = f32[1536,3,64]{0,2,1:T(8,128)} fusion(f32[3,512,1536]{2,1,0:T(8,128)} %fusion.251, f32[1536,3,64]{0,2,1:T(8,128)} %get-tuple-element.554, pred[]{:T(512)S(6)} %compare.3, bf16[1536,3,64]{0,2,1:T(8,128)(2,1)} %get-tuple-element.572, s32[]{:T(128)S(6)} %select_n.66, f32[3,512,1536]{2,1,0:T(8,128)} %get-tuple-element.471, ...), kind=kOutput, calls=%fused_computation.59.clone.1 | convolution fusion | flops 319097856 | bytes 40321028 | tf_op jit(solution)/shard_map/while/body/eval_jaxpr/hqk,qhd->khd/dot_general | solution.py:110
  422.8 15.3 %fusion.254 = (f32[3,512]{1,0:T(4,128)}, f32[3,512,1536]{2,1,0:T(8,128)}) fusion(f32[3,512,1536]{2,1,0:T(8,128)} %fusion.252, pred[512,1536]{1,0:T(8,128)(4,1)S(1)} %fusion.253), kind=kOutput, calls=%fused_computation.223.clone.1 | output fusion | flops 14157311 | bytes 19666944 | tf_op jit(solution)/shard_map/while/body/eval_jaxpr/sub | solution.py:52
  444.2 20.1 %fusion.257 = bf16[3,512,3,64]{1,3,2,0:T(8,128)(2,1)} fusion(bf16[3,512,3,64]{1,3,2,0:T(8,128)(2,1)} %get-tuple-element.556, s32[]{:T(128)} %get-tuple-element.553, bf16[1536,3,64]{0,2,1:T(8,128)(2,1)} %get-tuple-element.574, f32[3,512,1536]{2,1,0:T(8,128)} %fusion.251, f32[3,512,1536]{2,1,0:T(8,128)} %get-tuple-element.471, ...), kind=kOutput, calls=%fused_computation.61.clone.1 | convolution fusion | flops 318508032 | bytes 38748672 | tf_op jit(solution)/shard_map/while/body/eval_jaxpr/hqk,khd->qhd/dot_general | solution.py:113
  470.3 21.9 %fusion.255 = f32[1536,3,64]{0,2,1:T(8,128)} fusion(f32[3,512,1536]{2,1,0:T(8,128)} %fusion.251, f32[1536,3,64]{0,2,1:T(8,128)} %get-tuple-element.554, pred[]{:T(512)S(6)} %compare.3, bf16[1536,3,64]{0,2,1:T(8,128)(2,1)} %get-tuple-element.572, s32[]{:T(128)S(6)} %select_n.66, f32[3,512,1536]{2,1,0:T(8,128)} %get-tuple-element.471, ...), kind=kOutput, calls=%fused_computation.59.clone.1 | convolution fusion | flops 319097856 | bytes 40321028 | tf_op jit(solution)/shard_map/while/body/eval_jaxpr/hqk,qhd->khd/dot_general | solution.py:110
  506.0 75.5 %all_to_all.94 = bf16[1536,3,192]{2,1,0:T(4,128)(2,1)} all-to-all(bf16[1536,3,192]{2,1,0:T(4,128)(2,1)} %copy.104), channel_id=1, replica_groups=mesh['dp'=8,'head'=4] {'head'}, dimensions={0} | all-to-all | bytes 3538944 | tf_op jit(solution)/shard_map/all_to_all | solution.py:247
  587.1 6.8 convolution_multiply_fusion
  613.7 52.9 %all-to-all-done = bf16[384,3,768]{0,1,2:T(4,128)(2,1)} async-done(((bf16[384,3,768]{0,1,2:T(4,128)(2,1)}), bf16[384,3,768]{0,1,2:T(4,128)(2,1)}, u32[]{:S(2)}, u32[]{:S(2)}) %all-to-all-start) | async-done | bytes 1769504 | tf_op jit(solution)/shard_map/all_to_all | solution.py:157
  675.2 9.2 convolution_multiply_fusion.1
  688.6 91.5 %while.35 = (s32[]{:T(128)}, bf16[3,512,3,64]{1,3,2,0:T(8,128)(2,1)}, s32[3]{0:T(128)}, s32[1536]{0:T(1024)S(1)}, bf16[1536,3,64]{0,2,1:T(8,128)(2,1)}, /*index=...) while((s32[]{:T(128)}, ...), condition=%wide.region_7.8_spmd, body=%wide.region_4.7_spmd.sunk | while | flops 625215488 | bytes 43479760 | solution.py:80
  691.4 7.8 fusion.230
  699.2 14.7 %fusion.232 = (f32[3,512]{1,0:T(4,128)S(1)}, f32[3,512,1536]{2,1,0:T(8,128)}) fusion(f32[3,512,1536]{2,1,0:T(8,128)} %fusion.230, pred[512,1536]{1,0:T(8,128)(4,1)S(1)} %fusion.231), kind=kOutput, calls=%fused_computation.221.clone.1 | output fusion | flops 14157311 | bytes 19666944 | tf_op jit(solution)/shard_map/while/body/eval_jaxpr/sub | solution.py:52
  729.3 14.9 %fusion.232 = (f32[3,512]{1,0:T(4,128)S(1)}, f32[3,512,1536]{2,1,0:T(8,128)}) fusion(f32[3,512,1536]{2,1,0:T(8,128)} %fusion.230, pred[512,1536]{1,0:T(8,128)(4,1)S(1)} %fusion.231), kind=kOutput, calls=%fused_computation.221.clone.1 | output fusion | flops 14157311 | bytes 19666944 | tf_op jit(solution)/shard_map/while/body/eval_jaxpr/sub | solution.py:52
  759.4 14.7 %fusion.232 = (f32[3,512]{1,0:T(4,128)S(1)}, f32[3,512,1536]{2,1,0:T(8,128)}) fusion(f32[3,512,1536]{2,1,0:T(8,128)} %fusion.230, pred[512,1536]{1,0:T(8,128)(4,1)S(1)} %fusion.231), kind=kOutput, calls=%fused_computation.221.clone.1 | output fusion | flops 14157311 | bytes 19666944 | tf_op jit(solution)/shard_map/while/body/eval_jaxpr/sub | solution.py:52
  786.6 18.7 %all_to_all.95 = bf16[4,384,192]{1,2,0:T(8,128)(2,1)S(1)} all-to-all(bf16[4,384,192]{1,2,0:T(8,128)(2,1)S(1)} %copy.94), channel_id=1, replica_groups=mesh['dp'=8,'head'=4] {'head'}, dimensions={0} | all-to-all | bytes 1179648 | tf_op jit(solution)/shard_map/all_to_all | solution.py:165
  809.9 9.7 %fusion.111 = f32[384,768]{1,0:T(8,128)} fusion(f32[384,768]{1,0:T(8,128)} %copy-done.14, bf16[3072,768]{1,0:T(8,128)(2,1)} %param.35, bf16[768,3072]{1,0:T(8,128)(2,1)} %param.33, f32[3072]{0:T(1024)} %param.34, f32[768]{0:T(1024)} %param.36, f32[768]{0:T(1024)S(1)} %copy-done.22, f32[768]{0:T(1024)S(1)} %copy-done.18, f32[384]{0:T(512)} %add_rsqrt_fusion, ...), kind=kOutput, calls=%fused_computation.136 | convolution fusion | flops 3638034432 | bytes 11821056 | tf_op jit(solution)/shard_map/dot_general | solution.py:173
  840.4 42.1 %all-reduce = (f32[768]{0:T(1024)}, f32[768]{0:T(1024)}, f32[768]{0:T(1024)}, f32[768]{0:T(1024)}, f32[768]{0:T(1024)}, /*index=5*/f32[768]{0:T(1024)}, f32[768]{0:T(1024)}, f32[3072]{0:T(1024)}, f32[768]{0:T(1024)}) all-reduce(f32[768]{0:T(1024)} %get-tuple-element.311, ...), channel_id=1, replica_groups=mesh['dp'=8,'head'=4] {'dp','head'}, use_global_device_ids=true, to_apply=%region_28.29 | all-reduce | flops 9216 | bytes 73728 | tf_op jit(solution)/shard_map/psum | solution.py:269
  882.5 26.8 %all-reduce.4.cloned.1.call-done = (bf16[96,2304]{1,0:T(8,128)(2,1)}, bf16[96,768]{1,0:T(8,128)(2,1)}, bf16[768,384]{1,0:T(8,128)(2,1)}, bf16[384,768]{1,0:T(8,128)(2,1)}) async-done(((bf16[96,2304]{1,0:T(8,128)(2,1)}, bf16[96,768]{1,0:T(8,128)(2,1)}, bf16[768,384]{1,0:T(8,128)(2,1)}, bf16[384,768]{1,0:T(8,128)(2,1)}), (bf16[96,2304]{1,0:T(8,128)(2,1)}, bf16[96,768]{1,0:T(8,128)(2,1)}, ...) | async-done | bytes 1769488 | tf_op jit(solution)/shard_map/psum | solution.py:264
  (263 shorter events, 297.9 us)
Async XLA Ops:
  24.2 6.6 copy-start.40
  24.2 60.4 %all-to-all-start.2 = ((bf16[384,3,768]{0,1,2:T(4,128)(2,1)}), bf16[384,3,768]{0,1,2:T(4,128)(2,1)}, u32[]{:S(2)}, u32[]{:S(2)}) async-start(bf16[384,3,768]{0,1,2:T(4,128)(2,1)} %copy.96), calls=%async_computation.2 | async-start | bytes 4718592 | tf_op jit(solution)/shard_map/all_to_all | solution.py:157
  30.6 789.0 %reduce-scatter.7.cloned.1.call-start = ((), (), s32[]{:S(2)}) async-start(), calls=%async_computation.11 | async-start | bytes 2654208 | tf_op jit(solution)/shard_map/reduce_scatter | solution.py:259
  104.9 14.3 %copy-start.1 = (bf16[1536,3,64]{0,2,1:T(8,128)(2,1)S(1)}, bf16[1536,3,64]{0,2,1:T(8,128)(2,1)}, u32[]{:S(2)}) copy-start(bf16[1536,3,64]{0,2,1:T(8,128)(2,1)} %get-tuple-element.534) | copy-start | bytes 1769476 | tf_op jit(solution)/shard_map/while
  133.5 14.3 %copy-start.1 = (bf16[1536,3,64]{0,2,1:T(8,128)(2,1)S(1)}, bf16[1536,3,64]{0,2,1:T(8,128)(2,1)}, u32[]{:S(2)}) copy-start(bf16[1536,3,64]{0,2,1:T(8,128)(2,1)} %get-tuple-element.534) | copy-start | bytes 1769476 | tf_op jit(solution)/shard_map/while
  162.1 14.3 %copy-start.1 = (bf16[1536,3,64]{0,2,1:T(8,128)(2,1)S(1)}, bf16[1536,3,64]{0,2,1:T(8,128)(2,1)}, u32[]{:S(2)}) copy-start(bf16[1536,3,64]{0,2,1:T(8,128)(2,1)} %get-tuple-element.534) | copy-start | bytes 1769476 | tf_op jit(solution)/shard_map/while
  187.6 19.3 %copy-start.3 = (bf16[384,768]{1,0:T(8,128)(2,1)S(1)}, bf16[384,768]{1,0:T(8,128)(2,1)}, u32[]{:S(2)}) copy-start(bf16[384,768]{1,0:T(8,128)(2,1)} %param.22) | copy-start | bytes 1769476
  187.6 19.3 %copy-start.37 = (bf16[768,768]{1,0:T(8,128)(2,1)S(1)}, bf16[768,768]{1,0:T(8,128)(2,1)}, u32[]{:S(2)}) copy-start(bf16[768,768]{1,0:T(8,128)(2,1)} %param.29) | copy-start | bytes 3538948
  206.9 6.6 slice-start
  208.6 13.4 %copy-start.8 = (f32[384,768]{1,0:T(8,128)}, f32[384,768]{1,0:T(8,128)S(1)}, u32[]{:S(2)}) copy-start(f32[384,768]{1,0:T(8,128)S(1)} %get-tuple-element.299) | copy-start | bytes 3538948
  208.6 13.4 %copy-start.25 = (f32[384]{0:T(512)}, f32[384]{0:T(512)S(1)}, u32[]{:S(2)}) copy-start(f32[384]{0:T(512)S(1)} %broadcast_multiply_fusion.9) | copy-start | bytes 4612
  208.9 13.1 %copy-start.28 = (f32[384]{0:T(512)}, f32[384]{0:T(512)S(1)}, u32[]{:S(2)}) copy-start(f32[384]{0:T(512)S(1)} %fusion.146) | copy-start | bytes 4612
  208.9 10.2 %slice-start.2 = ((s8[4718592]{0:T(1024)(128)(4,1)}), s8[4194304]{0:T(1024)(128)(4,1)S(1)}, s32[]{:S(2)}) async-start(s8[4718592]{0:T(1024)(128)(4,1)} %bitcast.150), calls=%async_computation.17 | async-start | bytes 8388608
  213.6 5.5 copy-start.41
  213.6 5.5 slice-start.3
  231.4 19.4 %all-to-all-start.4 = ((bf16[384,4,192]{0,2,1:T(8,128)(2,1)}), bf16[384,4,192]{0,2,1:T(8,128)(2,1)}, u32[]{:S(2)}, u32[]{:S(2)}) async-start(bf16[384,4,192]{0,2,1:T(8,128)(2,1)} %bitcast.143), calls=%async_computation.4 | async-start | bytes 1179648 | tf_op jit(solution)/shard_map/all_to_all | solution.py:245
  235.6 590.6 %reduce-scatter.9.cloned.1.call-start = ((), (), s32[]{:S(2)}) async-start(), calls=%async_computation.12 | async-start | bytes 10616832 | tf_op jit(solution)/shard_map/reduce_scatter | solution.py:260
  244.4 583.9 %reduce-scatter.5.cloned.1.call-start = ((), (), s32[]{:S(2)}) async-start(), calls=%async_computation.10 | async-start | bytes 7962624 | tf_op jit(solution)/shard_map/reduce_scatter | solution.py:258
  265.1 16.7 %copy-start.2 = (bf16[1536,3,64]{0,2,1:T(8,128)(2,1)S(1)}, bf16[1536,3,64]{0,2,1:T(8,128)(2,1)}, u32[]{:S(2)}) copy-start(bf16[1536,3,64]{0,2,1:T(8,128)(2,1)} %get-tuple-element.576) | copy-start | bytes 1769476 | tf_op jit(solution)/shard_map/while
  344.9 15.3 %copy-start.2 = (bf16[1536,3,64]{0,2,1:T(8,128)(2,1)S(1)}, bf16[1536,3,64]{0,2,1:T(8,128)(2,1)}, u32[]{:S(2)}) copy-start(bf16[1536,3,64]{0,2,1:T(8,128)(2,1)} %get-tuple-element.576) | copy-start | bytes 1769476 | tf_op jit(solution)/shard_map/while
  422.8 15.3 %copy-start.2 = (bf16[1536,3,64]{0,2,1:T(8,128)(2,1)S(1)}, bf16[1536,3,64]{0,2,1:T(8,128)(2,1)}, u32[]{:S(2)}) copy-start(bf16[1536,3,64]{0,2,1:T(8,128)(2,1)} %get-tuple-element.576) | copy-start | bytes 1769476 | tf_op jit(solution)/shard_map/while
  581.5 5.6 copy-start.19
  581.5 5.6 copy-start.24
  609.2 57.4 %all-to-all-start = ((bf16[384,3,768]{0,1,2:T(4,128)(2,1)}), bf16[384,3,768]{0,1,2:T(4,128)(2,1)}, u32[]{:S(2)}, u32[]{:S(2)}) async-start(bf16[384,3,768]{0,1,2:T(4,128)(2,1)} %copy.90), calls=%async_computation | async-start | bytes 4718592 | tf_op jit(solution)/shard_map/all_to_all | solution.py:157
  613.7 216.6 %reduce-scatter.11.cloned.1.call-start = ((), (), s32[]{:S(2)}) async-start(), calls=%async_computation.13 | async-start | bytes 10616832 | tf_op jit(solution)/shard_map/reduce_scatter | solution.py:261
  684.5 224.9 %all-reduce.4.cloned.1.call-start = ((), (), s32[]{:S(2)}) async-start(), calls=%async_computation.14 | async-start | bytes 3538944 | tf_op jit(solution)/shard_map/psum | solution.py:264
  699.2 14.7 %copy-start.15 = (bf16[1536,3,64]{0,2,1:T(8,128)(2,1)S(1)}, bf16[1536,3,64]{0,2,1:T(8,128)(2,1)}, u32[]{:S(2)}) copy-start(bf16[1536,3,64]{0,2,1:T(8,128)(2,1)} %get-tuple-element.501) | copy-start | bytes 1769476 | tf_op jit(solution)/shard_map/while
  729.3 14.9 %copy-start.15 = (bf16[1536,3,64]{0,2,1:T(8,128)(2,1)S(1)}, bf16[1536,3,64]{0,2,1:T(8,128)(2,1)}, u32[]{:S(2)}) copy-start(bf16[1536,3,64]{0,2,1:T(8,128)(2,1)} %get-tuple-element.501) | copy-start | bytes 1769476 | tf_op jit(solution)/shard_map/while
  759.4 14.7 %copy-start.15 = (bf16[1536,3,64]{0,2,1:T(8,128)(2,1)S(1)}, bf16[1536,3,64]{0,2,1:T(8,128)(2,1)}, u32[]{:S(2)}) copy-start(bf16[1536,3,64]{0,2,1:T(8,128)(2,1)} %get-tuple-element.501) | copy-start | bytes 1769476 | tf_op jit(solution)/shard_map/while
  785.3 19.9 %copy-start.4 = (bf16[384,768]{1,0:T(8,128)(2,1)S(1)}, bf16[384,768]{1,0:T(8,128)(2,1)}, u32[]{:S(2)}) copy-start(bf16[384,768]{1,0:T(8,128)(2,1)} %param.22) | copy-start | bytes 1769476
  785.3 19.9 %copy-start.38 = (bf16[768,768]{1,0:T(8,128)(2,1)S(1)}, bf16[768,768]{1,0:T(8,128)(2,1)}, u32[]{:S(2)}) copy-start(bf16[768,768]{1,0:T(8,128)(2,1)} %param.29) | copy-start | bytes 3538948
  909.4 5.3 copy-start.20
  (28 other events, 85.7 us)
Sparse Core Ops, SparseCore 0:
  226.1 41.5 reduce-scatter.6
  271.6 76.5 reduce-scatter.8
  594.0 64.2 reduce-scatter.4
  684.6 75.2 reduce-scatter.10
  832.6 76.7 all-reduce.3
where the time goes:
time: 929 us; the launch traced here: 922 us
  matrix products  327 us (35%)
  other arithmetic  176 us (19%)
  blocking collectives  154 us (17%)
  waiting for transfers between devices  140 us (15%)
  local copies, waits for them, and re-layouts  89.2 us (10%)
  starting transfers between devices  15.4 us (2%)
  between operations  14.8 us (2%)
    sub x9, other arithmetic, block_weights(): weights = jnp.exp(scores - largest)  134 us
    all_to_all x2, waiting for transfers between devices, forward(): lax.all_to_all(mixed_rows.reshape(tok_rows, 3, model_width), 'head', spli...  106 us
    all_to_all x1, blocking collectives, shards(): lax.all_to_all(group_mixed_grad, 'head', split_axis=0, concat_axis=2, til...  75.5 us
    dot_general x3, matrix products, one_block(): jnp.einsum('hqk,qhd->khd', score_grad, query_block, preferred_element_typ...  65.4 us
    dot_general x3, matrix products, one_block(): jnp.einsum('hqk,khd->qhd', score_grad, key_heads, preferred_element_type=...  60.3 us
    dot_general x9, matrix products, block_weights(): jnp.einsum('qhd,khd->hqk', query_block, key_heads, preferred_element_type...  58.2 us
    psum x1, blocking collectives, shards(): lax.psum((grad_ln1_gain * grad_scale, grad_ln1_bias * grad_scale, grad_bi...  42.1 us
    all_to_all x2, blocking collectives, forward(): lax.all_to_all(attended, 'head', split_axis=0, concat_axis=1, tiled=True)  36.7 us
  transfers between devices with their start and end apart: 8, of which 4 were waited for; matrix products, arithmetic and copies ran while one was open for 48% of the time, Pallas kernels for 0%

commit v1 on v0

--- a/solution.py
+++ b/solution.py
@@ -219,11 +219,7 @@
     )
     kept = forward(tokens, seq_ids, weight_set)
     block_output = kept[8]
-    fresh_tokens, fresh_weights, fresh_grad = lax.optimization_barrier(
-        (tokens, weight_set, cotangent)
-    )
-    kept = forward(fresh_tokens, seq_ids, fresh_weights)
-    grad_rows = fresh_grad.astype(jnp.float32)
+    grad_rows = cotangent.astype(jnp.float32)
     source, normed, group_mixed, back_rows, middle, second, pre_act, hidden, result = kept
     grad_bias_proj = DEPTH_SCALE * jnp.sum(grad_rows, axis=0)
     proj_grad = (DEPTH_SCALE * grad_rows).astype(jnp.bfloat16)
@@ -255,10 +251,10 @@
     token_part, grad_ln1_gain, grad_ln1_bias = first_pull(normed_grad)
     grad_tokens = middle_grad + token_part
     mat_shares = (
-        lax.psum_scatter(grad_w_qkv * grad_scale, "dp", scatter_dimension=0, tiled=True),
-        lax.psum_scatter(grad_w_out * grad_scale, "dp", scatter_dimension=0, tiled=True),
-        lax.psum_scatter(grad_w_fc * grad_scale, "dp", scatter_dimension=1, tiled=True),
-        lax.psum_scatter(grad_w_proj * grad_scale, "dp", scatter_dimension=0, tiled=True),
+        lax.psum_scatter((grad_w_qkv * grad_scale).astype(jnp.bfloat16), "dp", scatter_dimension=0, tiled=True),
+        lax.psum_scatter((grad_w_out * grad_scale).astype(jnp.bfloat16), "dp", scatter_dimension=0, tiled=True),
+        lax.psum_scatter((grad_w_fc * grad_scale).astype(jnp.bfloat16), "dp", scatter_dimension=1, tiled=True),
+        lax.psum_scatter((grad_w_proj * grad_scale).astype(jnp.bfloat16), "dp", scatter_dimension=0, tiled=True),
     )
     qkv_total, out_total, fc_total, proj_total = (
         lax.psum(mat_shares[0].astype(jnp.bfloat16), "head").astype(jnp.float32),

time: 929 us -> 753 us (0.81)
  other arithmetic: 176 us -> 116 us
  matrix products: 327 us -> 276 us
  local copies, waits for them, and re-layouts: 89.2 us -> 67.3 us
  waiting for transfers between devices: 140 us -> 120 us
  blocking collectives: 154 us -> 137 us
    all_to_all x2 -> x1, waiting for transfers between devices: 106 us -> 53.5 us  [forward(): lax.all_to_all(mixed_rows.reshape(tok_rows, 3, model_width), 'head', spli...]
    sub x9 -> x6, other arithmetic: 134 us -> 87.8 us  [block_weights(): weights = jnp.exp(scores - largest)]
    reduce_scatter x4 -> x3, waiting for transfers between devices: 0.01 us -> 31.4 us  [the longest x1 31.4 us: shards(): lax.psum_scatter((grad_w_qkv * grad_scale).astype(jnp.bfloat16), 'dp', sc...]
    dot_general x9 -> x6, matrix products: 58.2 us -> 37.7 us  [block_weights(): jnp.einsum('qhd,khd->hqk', query_block, key_heads, preferred_element_type...]
    all_to_all x2 -> x1, blocking collectives: 36.7 us -> 18.2 us  [forward(): lax.all_to_all(attended, 'head', split_axis=0, concat_axis=1, tiled=True)]
    dot_general x6 -> x3, matrix products: 36.3 us -> 18 us  [one_block(): jnp.einsum('hqk,khd->qhd', soft_weights.astype(jnp.bfloat16), value_heads...]
    unnamed x86 -> x94, local copies, waits for them, and re-layouts: 3 us -> 12.9 us
  transfers between devices with their start and end apart: 8 -> 7, of which waited for: 4 -> 4; matrix products, arithmetic and copies ran while one was open for 48% -> 41% of each run, Pallas kernels for 0% -> 0%
where the time goes in v1:
time: 753 us; the launch traced here: 747 us
  matrix products  276 us (37%)
  blocking collectives  137 us (18%)
  waiting for transfers between devices  120 us (16%)
  other arithmetic  116 us (15%)
  local copies, waits for them, and re-layouts  67.3 us (9%)
  between operations  14.5 us (2%)
  starting transfers between devices  10.9 us (1%)
    sub x6, other arithmetic, block_weights(): weights = jnp.exp(scores - largest)  87.8 us
    all_to_all x1, blocking collectives, shards(): lax.all_to_all(group_mixed_grad, 'head', split_axis=0, concat_axis=2, til...  75.6 us
    dot_general x3, matrix products, one_block(): jnp.einsum('hqk,qhd->khd', score_grad, query_block, preferred_element_typ...  66 us
    dot_general x3, matrix products, one_block(): jnp.einsum('hqk,khd->qhd', score_grad, key_heads, preferred_element_type=...  60.9 us
    all_to_all x1, waiting for transfers between devices, forward(): lax.all_to_all(mixed_rows.reshape(tok_rows, 3, model_width), 'head', spli...  53.5 us
    psum x1, blocking collectives, shards(): lax.psum((grad_ln1_gain * grad_scale, grad_ln1_bias * grad_scale, grad_bi...  43.3 us
    dot_general x6, matrix products, block_weights(): jnp.einsum('qhd,khd->hqk', query_block, key_heads, preferred_element_type...  37.7 us
    reduce_scatter x1, waiting for transfers between devices, shards(): lax.psum_scatter((grad_w_qkv * grad_scale).astype(jnp.bfloat16), 'dp', sc...  31.4 us
  transfers between devices with their start and end apart: 7, of which 4 were waited for; matrix products, arithmetic and copies ran while one was open for 41% of the time, Pallas kernels for 0%

profile of v1, /device:TPU:0, one launch (start us, length us, event | category | flops | bytes accessed | tf_op | source)
XLA Modules:
  0.0 746.9 jit_solution(16026137522256151218)
XLA Ops:
  23.5 6.4 all-to-all-start
  30.4 53.5 %all-to-all-done = bf16[384,3,768]{0,1,2:T(4,128)(2,1)} async-done(((bf16[384,3,768]{0,1,2:T(4,128)(2,1)}), bf16[384,3,768]{0,1,2:T(4,128)(2,1)}, u32[]{:S(2)}, u32[]{:S(2)}) %all-to-all-start) | async-done | bytes 1769504 | tf_op jit(solution)/shard_map/all_to_all | solution.py:157
  95.8 85.8 %while.25 = (s32[]{:T(128)}, bf16[3,512,3,64]{1,3,2,0:T(8,128)(2,1)}, s32[3]{0:T(128)S(1)}, s32[1536]{0:T(1024)S(1)}, bf16[1536,3,64]{0,2,1:T(8,128)(2,1)}, /*in...) while((s32[]{:T(128)}, ...), condition=%wide.region_7.8_spmd, body=%wide.region_4.7_spmd.sunk | while | flops 625215488 | bytes 43479760 | solution.py:80
  98.0 6.2 fusion.158
  104.2 14.3 %fusion.160 = (f32[3,512]{1,0:T(4,128)S(1)}, f32[3,512,1536]{2,1,0:T(8,128)}) fusion(f32[3,512,1536]{2,1,0:T(8,128)} %fusion.158, pred[512,1536]{1,0:T(8,128)(4,1)S(1)} %fusion.159), kind=kOutput, calls=%fused_computation.148.clone.1 | output fusion | flops 14157311 | bytes 19666944 | tf_op jit(solution)/shard_map/while/body/eval_jaxpr/sub | solution.py:52
  126.6 6.2 fusion.158
  132.8 14.3 %fusion.160 = (f32[3,512]{1,0:T(4,128)S(1)}, f32[3,512,1536]{2,1,0:T(8,128)}) fusion(f32[3,512,1536]{2,1,0:T(8,128)} %fusion.158, pred[512,1536]{1,0:T(8,128)(4,1)S(1)} %fusion.159), kind=kOutput, calls=%fused_computation.148.clone.1 | output fusion | flops 14157311 | bytes 19666944 | tf_op jit(solution)/shard_map/while/body/eval_jaxpr/sub | solution.py:52
  155.2 6.2 fusion.158
  161.4 14.3 %fusion.160 = (f32[3,512]{1,0:T(4,128)S(1)}, f32[3,512,1536]{2,1,0:T(8,128)}) fusion(f32[3,512,1536]{2,1,0:T(8,128)} %fusion.158, pred[512,1536]{1,0:T(8,128)(4,1)S(1)} %fusion.159), kind=kOutput, calls=%fused_computation.148.clone.1 | output fusion | flops 14157311 | bytes 19666944 | tf_op jit(solution)/shard_map/while/body/eval_jaxpr/sub | solution.py:52
  188.2 18.2 %all_to_all.62 = bf16[4,384,192]{1,2,0:T(8,128)(2,1)S(1)} all-to-all(bf16[4,384,192]{1,2,0:T(8,128)(2,1)S(1)} %copy.74), channel_id=1, replica_groups=mesh['dp'=8,'head'=4] {'head'}, dimensions={0} | all-to-all | bytes 1179648 | tf_op jit(solution)/shard_map/all_to_all | solution.py:165
  224.5 6.7 copy.83
  231.3 6.3 multiply_reduce_fusion.1
  251.1 8.3 %multiply_convert_fusion.1 = bf16[3072,768]{1,0:T(8,128)(2,1)} fusion(bf16[384,768]{1,0:T(8,128)(2,1)} %param.35, f32[384,3072]{1,0:T(8,128)} %copy-done.45), kind=kOutput, calls=%fused_computation.60 | convolution fusion | flops 1828159488 | bytes 10027008 | tf_op jit(solution)/shard_map/dot_general | solution.py:23
  259.5 6.8 all-to-all-done.2
  271.8 233.5 %while.26 = (s32[]{:T(128)}, f32[1536,3,64]{0,2,1:T(8,128)}, f32[1536,3,64]{0,2,1:T(8,128)}, bf16[3,512,3,64]{1,3,2,0:T(8,128)(2,1)}, s32[3]{0:T(128)S(1)}, /*in...) while((s32[]{:T(128)}, f32[1536,3,64]{0,2,1:T(8,128)}, ...), condition=%wide.region_16.17_spmd.clone, body=%wide.region_12.16_spmd.clone.sunk | while | flops 1565401088 | bytes 134347520 | solution.py:119
  274.1 6.4 fusion.173
  280.6 15.0 %fusion.175 = (f32[3,512]{1,0:T(4,128)}, f32[3,512,1536]{2,1,0:T(8,128)}) fusion(f32[3,512,1536]{2,1,0:T(8,128)} %fusion.173, pred[512,1536]{1,0:T(8,128)(4,1)S(1)} %fusion.174), kind=kOutput, calls=%fused_computation.149.clone.1 | output fusion | flops 14157311 | bytes 19666944 | tf_op jit(solution)/shard_map/while/body/eval_jaxpr/sub | solution.py:52
  301.6 20.3 %fusion.178 = bf16[3,512,3,64]{1,3,2,0:T(8,128)(2,1)} fusion(bf16[3,512,3,64]{1,3,2,0:T(8,128)(2,1)} %get-tuple-element.389, s32[]{:T(128)} %get-tuple-element.386, bf16[1536,3,64]{0,2,1:T(8,128)(2,1)} %get-tuple-element.407, f32[3,512,1536]{2,1,0:T(8,128)} %fusion.172, f32[3,512,1536]{2,1,0:T(8,128)} %get-tuple-element.337, ...), kind=kOutput, calls=%fused_computation.42.clone.1 | convolution fusion | flops 318508032 | bytes 38748672 | tf_op jit(solution)/shard_map/while/body/eval_jaxpr/hqk,khd->qhd/dot_general | solution.py:113
  327.7 21.8 %fusion.176 = f32[1536,3,64]{0,2,1:T(8,128)} fusion(f32[3,512,1536]{2,1,0:T(8,128)} %fusion.172, f32[1536,3,64]{0,2,1:T(8,128)} %get-tuple-element.387, pred[]{:T(512)S(6)} %compare.3, bf16[1536,3,64]{0,2,1:T(8,128)(2,1)} %get-tuple-element.405, s32[]{:T(128)S(6)} %select_n.45, f32[3,512,1536]{2,1,0:T(8,128)} %get-tuple-element.337, ...), kind=kOutput, calls=%fused_computation.40.clone.1 | convolution fusion | flops 319097856 | bytes 40321028 | tf_op jit(solution)/shard_map/while/body/eval_jaxpr/hqk,qhd->khd/dot_general | solution.py:110
  351.5 6.3 fusion.173
  357.8 15.0 %fusion.175 = (f32[3,512]{1,0:T(4,128)}, f32[3,512,1536]{2,1,0:T(8,128)}) fusion(f32[3,512,1536]{2,1,0:T(8,128)} %fusion.173, pred[512,1536]{1,0:T(8,128)(4,1)S(1)} %fusion.174), kind=kOutput, calls=%fused_computation.149.clone.1 | output fusion | flops 14157311 | bytes 19666944 | tf_op jit(solution)/shard_map/while/body/eval_jaxpr/sub | solution.py:52
  378.8 20.3 %fusion.178 = bf16[3,512,3,64]{1,3,2,0:T(8,128)(2,1)} fusion(bf16[3,512,3,64]{1,3,2,0:T(8,128)(2,1)} %get-tuple-element.389, s32[]{:T(128)} %get-tuple-element.386, bf16[1536,3,64]{0,2,1:T(8,128)(2,1)} %get-tuple-element.407, f32[3,512,1536]{2,1,0:T(8,128)} %fusion.172, f32[3,512,1536]{2,1,0:T(8,128)} %get-tuple-element.337, ...), kind=kOutput, calls=%fused_computation.42.clone.1 | convolution fusion | flops 318508032 | bytes 38748672 | tf_op jit(solution)/shard_map/while/body/eval_jaxpr/hqk,khd->qhd/dot_general | solution.py:113
  405.2 22.1 %fusion.176 = f32[1536,3,64]{0,2,1:T(8,128)} fusion(f32[3,512,1536]{2,1,0:T(8,128)} %fusion.172, f32[1536,3,64]{0,2,1:T(8,128)} %get-tuple-element.387, pred[]{:T(512)S(6)} %compare.3, bf16[1536,3,64]{0,2,1:T(8,128)(2,1)} %get-tuple-element.405, s32[]{:T(128)S(6)} %select_n.45, f32[3,512,1536]{2,1,0:T(8,128)} %get-tuple-element.337, ...), kind=kOutput, calls=%fused_computation.40.clone.1 | convolution fusion | flops 319097856 | bytes 40321028 | tf_op jit(solution)/shard_map/while/body/eval_jaxpr/hqk,qhd->khd/dot_general | solution.py:110
  429.4 6.3 fusion.173
  435.7 15.0 %fusion.175 = (f32[3,512]{1,0:T(4,128)}, f32[3,512,1536]{2,1,0:T(8,128)}) fusion(f32[3,512,1536]{2,1,0:T(8,128)} %fusion.173, pred[512,1536]{1,0:T(8,128)(4,1)S(1)} %fusion.174), kind=kOutput, calls=%fused_computation.149.clone.1 | output fusion | flops 14157311 | bytes 19666944 | tf_op jit(solution)/shard_map/while/body/eval_jaxpr/sub | solution.py:52
  456.7 20.3 %fusion.178 = bf16[3,512,3,64]{1,3,2,0:T(8,128)(2,1)} fusion(bf16[3,512,3,64]{1,3,2,0:T(8,128)(2,1)} %get-tuple-element.389, s32[]{:T(128)} %get-tuple-element.386, bf16[1536,3,64]{0,2,1:T(8,128)(2,1)} %get-tuple-element.407, f32[3,512,1536]{2,1,0:T(8,128)} %fusion.172, f32[3,512,1536]{2,1,0:T(8,128)} %get-tuple-element.337, ...), kind=kOutput, calls=%fused_computation.42.clone.1 | convolution fusion | flops 318508032 | bytes 38748672 | tf_op jit(solution)/shard_map/while/body/eval_jaxpr/hqk,khd->qhd/dot_general | solution.py:113
  483.1 22.1 %fusion.176 = f32[1536,3,64]{0,2,1:T(8,128)} fusion(f32[3,512,1536]{2,1,0:T(8,128)} %fusion.172, f32[1536,3,64]{0,2,1:T(8,128)} %get-tuple-element.387, pred[]{:T(512)S(6)} %compare.3, bf16[1536,3,64]{0,2,1:T(8,128)(2,1)} %get-tuple-element.405, s32[]{:T(128)S(6)} %select_n.45, f32[3,512,1536]{2,1,0:T(8,128)} %get-tuple-element.337, ...), kind=kOutput, calls=%fused_computation.40.clone.1 | convolution fusion | flops 319097856 | bytes 40321028 | tf_op jit(solution)/shard_map/while/body/eval_jaxpr/hqk,qhd->khd/dot_general | solution.py:110
  519.0 75.6 %all_to_all.63 = bf16[1536,3,192]{2,1,0:T(4,128)(2,1)} all-to-all(bf16[1536,3,192]{2,1,0:T(4,128)(2,1)} %copy.78), channel_id=1, replica_groups=mesh['dp'=8,'head'=4] {'head'}, dimensions={0} | all-to-all | bytes 3538944 | tf_op jit(solution)/shard_map/all_to_all | solution.py:243
  607.9 8.4 %fusion.81 = f32[384,768]{1,0:T(8,128)} fusion(f32[384,768]{1,0:T(8,128)} %copy-done.10, bf16[3072,768]{1,0:T(8,128)(2,1)} %param.33, f32[768]{0:T(1024)} %param.34, f32[384,3072]{1,0:T(8,128)} %copy-done.45), kind=kOutput, calls=%fused_computation.95 | convolution fusion | flops 1823440896 | bytes 11799552 | tf_op jit(solution)/shard_map/dot_general | solution.py:173
  621.8 31.4 %reduce-scatter.7.cloned.1.call-done = bf16[96,2304]{1,0:T(8,128)(2,1)} async-done(((bf16[768,2304]{1,0:T(8,128)(2,1)}), bf16[96,2304]{1,0:T(8,128)(2,1)}) %reduce-scatter.7.cloned.1.call-update) | async-done | bytes 442384 | tf_op jit(solution)/shard_map/reduce_scatter | solution.py:254
  662.3 43.3 %all-reduce = (f32[768]{0:T(1024)}, f32[768]{0:T(1024)}, f32[768]{0:T(1024)}, f32[768]{0:T(1024)}, f32[768]{0:T(1024)}, /*index=5*/f32[768]{0:T(1024)}, f32[768]{0:T(1024)}, f32[3072]{0:T(1024)}, f32[768]{0:T(1024)}) all-reduce(f32[768]{0:T(1024)} %get-tuple-element.224, ...), channel_id=1, replica_groups=mesh['dp'=8,'head'=4] {'dp','head'}, use_global_device_ids=true, to_apply=%region_20.21 | all-reduce | flops 9216 | bytes 73728 | tf_op jit(solution)/shard_map/psum | solution.py:265
  705.7 28.4 %all-reduce.4.cloned.1.call-done = (bf16[96,2304]{1,0:T(8,128)(2,1)}, bf16[96,768]{1,0:T(8,128)(2,1)}, bf16[768,384]{1,0:T(8,128)(2,1)}, bf16[384,768]{1,0:T(8,128)(2,1)}) async-done(((bf16[96,2304]{1,0:T(8,128)(2,1)}, bf16[96,768]{1,0:T(8,128)(2,1)}, bf16[768,384]{1,0:T(8,128)(2,1)}, bf16[384,768]{1,0:T(8,128)(2,1)}), (bf16[96,2304]{1,0:T(8,128)(2,1)}, bf16[96,768]{1,0:T(8,128)(2,1)}, ...) | async-done | bytes 1769488 | tf_op jit(solution)/shard_map/psum | solution.py:260
  (215 shorter events, 182.4 us)
Async XLA Ops:
  23.5 6.6 copy-start.43
  23.5 60.4 %all-to-all-start = ((bf16[384,3,768]{0,1,2:T(4,128)(2,1)}), bf16[384,3,768]{0,1,2:T(4,128)(2,1)}, u32[]{:S(2)}, u32[]{:S(2)}) async-start(bf16[384,3,768]{0,1,2:T(4,128)(2,1)} %copy.70), calls=%async_computation | async-start | bytes 4718592 | tf_op jit(solution)/shard_map/all_to_all | solution.py:157
  30.0 589.7 %reduce-scatter.13.cloned.1.call-start = ((), (), s32[]{:S(2)}) async-start(), calls=%async_computation.11 | async-start | bytes 5308416
  104.2 14.3 %copy-start.1 = (bf16[1536,3,64]{0,2,1:T(8,128)(2,1)S(1)}, bf16[1536,3,64]{0,2,1:T(8,128)(2,1)}, u32[]{:S(2)}) copy-start(bf16[1536,3,64]{0,2,1:T(8,128)(2,1)} %get-tuple-element.367) | copy-start | bytes 1769476 | tf_op jit(solution)/shard_map/while
  132.8 14.3 %copy-start.1 = (bf16[1536,3,64]{0,2,1:T(8,128)(2,1)S(1)}, bf16[1536,3,64]{0,2,1:T(8,128)(2,1)}, u32[]{:S(2)}) copy-start(bf16[1536,3,64]{0,2,1:T(8,128)(2,1)} %get-tuple-element.367) | copy-start | bytes 1769476 | tf_op jit(solution)/shard_map/while
  161.4 14.3 %copy-start.1 = (bf16[1536,3,64]{0,2,1:T(8,128)(2,1)S(1)}, bf16[1536,3,64]{0,2,1:T(8,128)(2,1)}, u32[]{:S(2)}) copy-start(bf16[1536,3,64]{0,2,1:T(8,128)(2,1)} %get-tuple-element.367) | copy-start | bytes 1769476 | tf_op jit(solution)/shard_map/while
  181.7 24.7 %copy-start.40 = (f32[768]{0:T(1024)S(1)}, f32[768]{0:T(1024)}, u32[]{:S(2)}) copy-start(f32[768]{0:T(1024)} %param.28) | copy-start | bytes 9220
  186.9 19.5 %copy-start.5 = (bf16[384,768]{1,0:T(8,128)(2,1)S(1)}, bf16[384,768]{1,0:T(8,128)(2,1)}, u32[]{:S(2)}) copy-start(bf16[384,768]{1,0:T(8,128)(2,1)} %param.20) | copy-start | bytes 1769476
  186.9 19.5 %copy-start.38 = (bf16[768,768]{1,0:T(8,128)(2,1)S(1)}, bf16[768,768]{1,0:T(8,128)(2,1)}, u32[]{:S(2)}) copy-start(bf16[768,768]{1,0:T(8,128)(2,1)} %param.27) | copy-start | bytes 3538948
  206.4 6.4 slice-start
  207.2 11.1 %copy-start.10 = (f32[384,768]{1,0:T(8,128)}, f32[384,768]{1,0:T(8,128)S(1)}, u32[]{:S(2)}) copy-start(f32[384,768]{1,0:T(8,128)S(1)} %get-tuple-element.212) | copy-start | bytes 3538948
  207.6 10.8 %copy-start.31 = (f32[384]{0:T(512)}, f32[384]{0:T(512)S(1)}, u32[]{:S(2)}) copy-start(f32[384]{0:T(512)S(1)} %fusion.97) | copy-start | bytes 4612
  212.9 5.5 copy-start.45
  231.2 390.6 %reduce-scatter.9.cloned.1.call-start = ((), (), s32[]{:S(2)}) async-start(), calls=%async_computation.9 | async-start | bytes 1327104 | tf_op jit(solution)/shard_map/reduce_scatter | solution.py:255
  231.2 6.4 copy-start.11
  231.3 6.4 copy-start.32
  231.3 6.4 copy-start.37
  246.9 19.4 %all-to-all-start.2 = ((bf16[384,4,192]{0,2,1:T(8,128)(2,1)}), bf16[384,4,192]{0,2,1:T(8,128)(2,1)}, u32[]{:S(2)}, u32[]{:S(2)}) async-start(bf16[384,4,192]{0,2,1:T(8,128)(2,1)} %bitcast.106), calls=%async_computation.2 | async-start | bytes 1179648 | tf_op jit(solution)/shard_map/all_to_all | solution.py:241
  251.1 370.7 %reduce-scatter.11.cloned.1.call-start = ((), (), s32[]{:S(2)}) async-start(), calls=%async_computation.10 | async-start | bytes 5308416 | tf_op jit(solution)/shard_map/reduce_scatter | solution.py:257
  259.5 393.7 %reduce-scatter.7.cloned.1.call-start = ((), (), s32[]{:S(2)}) async-start(), calls=%async_computation.8 | async-start | bytes 3981312 | tf_op jit(solution)/shard_map/reduce_scatter | solution.py:254
  280.6 15.0 %copy-start.2 = (bf16[1536,3,64]{0,2,1:T(8,128)(2,1)S(1)}, bf16[1536,3,64]{0,2,1:T(8,128)(2,1)}, u32[]{:S(2)}) copy-start(bf16[1536,3,64]{0,2,1:T(8,128)(2,1)} %get-tuple-element.409) | copy-start | bytes 1769476 | tf_op jit(solution)/shard_map/while
  357.8 15.0 %copy-start.2 = (bf16[1536,3,64]{0,2,1:T(8,128)(2,1)S(1)}, bf16[1536,3,64]{0,2,1:T(8,128)(2,1)}, u32[]{:S(2)}) copy-start(bf16[1536,3,64]{0,2,1:T(8,128)(2,1)} %get-tuple-element.409) | copy-start | bytes 1769476 | tf_op jit(solution)/shard_map/while
  435.7 15.0 %copy-start.2 = (bf16[1536,3,64]{0,2,1:T(8,128)(2,1)S(1)}, bf16[1536,3,64]{0,2,1:T(8,128)(2,1)}, u32[]{:S(2)}) copy-start(bf16[1536,3,64]{0,2,1:T(8,128)(2,1)} %get-tuple-element.409) | copy-start | bytes 1769476 | tf_op jit(solution)/shard_map/while
  594.6 5.6 copy-start.21
  594.6 5.6 copy-start.23
  594.6 5.6 copy-start.28
  594.6 5.6 copy-start.42
  605.9 128.1 %all-reduce.4.cloned.1.call-start = ((), (), s32[]{:S(2)}) async-start(), calls=%async_computation.12 | async-start | bytes 3538944 | tf_op jit(solution)/shard_map/psum | solution.py:260
  607.9 8.4 %copy-start.6 = (bf16[384,768]{1,0:T(8,128)(2,1)S(1)}, bf16[384,768]{1,0:T(8,128)(2,1)}, u32[]{:S(2)}) copy-start(bf16[384,768]{1,0:T(8,128)(2,1)} %param.20) | copy-start | bytes 1769476
  607.9 8.4 %copy-start.8 = (bf16[384,3,4,192]{0,3,2,1:T(8,128)(2,1)S(1)}, bf16[384,3,4,192]{0,3,2,1:T(8,128)(2,1)}, u32[]{:S(2)}) copy-start(bf16[384,3,4,192]{0,3,2,1:T(8,128)(2,1)} %copy.80) | copy-start | bytes 5308420
  607.9 8.4 %copy-start.29 = (f32[768]{0:T(1024)S(1)}, f32[768]{0:T(1024)}, u32[]{:S(2)}) copy-start(f32[768]{0:T(1024)} %param.22) | copy-start | bytes 9220
  734.1 5.3 copy-start.19
  (27 other events, 72.0 us)
Sparse Core Ops, SparseCore 0:
  231.3 52.9 reduce-scatter.12
  287.9 36.7 reduce-scatter.8
  328.2 53.8 reduce-scatter.10
  606.1 47.0 reduce-scatter.6
  656.4 77.5 all-reduce.3

commit v2 on v1

v2 whole, which is shorter than its diff:
```python
import functools
import math

import jax
import jax.numpy as jnp
from jax import lax
from jax.experimental import pallas as pl
from jax.experimental.pallas import tpu as pltpu
from jax.sharding import PartitionSpec as P

HEAD_DIM = 64
EPSILON = 1e-05
DEPTH_SCALE = 1.0 / math.sqrt(12.0)
LOG2E = 1.0 / math.log(2.0)
SCORE_SCALE = HEAD_DIM ** (-0.5)
GELU_K = math.sqrt(2.0 / math.pi)
GELU_A = 0.044715
TEAM = 8
QB = 256

F32 = jnp.float32
BF16 = jnp.bfloat16
MESH = pl.DeviceIdType.MESH
ANY = pl.BlockSpec(memory_space=pl.ANY)
VMEM = pl.BlockSpec(memory_space=pltpu.VMEM)
SMEM = pl.BlockSpec(memory_space=pltpu.SMEM)


def dot(a, b):
    return jnp.dot(a, b, preferred_element_type=F32)


def dot_nt(a, b):
    return lax.dot_general(a, b, (((1,), (1,)), ((), ())), preferred_element_type=F32)


def dot_tn(a, b):
    return lax.dot_general(a, b, (((0,), (0,)), ((), ())), preferred_element_type=F32)


def mult(x, m):
    return pl.multiple_of(x, m)


def place():
    dp, h = lax.axis_index("dp"), lax.axis_index("head")
    core = lax.rem(dp, 2)
    half = h // 2
    return dict(
        dp=dp,
        h=h,
        core=core,
        sib=dp + 1 - 2 * core,
        even=dp - core,
        half=half,
        served=dp - core + half,
        block=(h - 2 * half) * 2 + core,
    )


def greet(at):
    barrier = pltpu.get_barrier_semaphore()
    me = at["core"] * 4 + at["h"]
    for k in range(1, TEAM):
        other = lax.rem(me + k, TEAM)
        pl.semaphore_signal(
            barrier, inc=1, device_id=(at["even"] + other // 4, lax.rem(other, 4)), device_id_type=MESH
        )
    pl.semaphore_wait(barrier, TEAM - 1)


def remote(src, dst, send, recv, device):
    return pltpu.make_async_remote_copy(
        src_ref=src, dst_ref=dst, send_sem=send, recv_sem=recv, device_id=device, device_id_type=MESH
    )


def norm_parts(v):
    center = jnp.mean(v, axis=-1, keepdims=True)
    cent = v - center
    r = lax.rsqrt(jnp.mean(cent * cent, axis=-1, keepdims=True) + EPSILON)
    return cent * r, r


def norm_back(e, gain, n, r):
    ea = e * gain
    return r * (ea - jnp.mean(ea, axis=-1, keepdims=True) - n * jnp.mean(ea * n, axis=-1, keepdims=True))


def attend_kernel(
    tok, lens, gain, bias, bias_q, bias_v, w_qkv,
    att_o, mix_o, xg_o, ot_o, lse_o, start_o, wt_o,
    xn, xg, wwin, tbuf, wt, bcol, start_mine, start_sib, mix, kh, scores, ot,
    w_sem, st_sem, ag_send, ag_recv, fw_send, at_send, at_recv, at_local, out_sem,
):
    at = place()
    dp, h, core, sib = at["dp"], at["h"], at["core"], at["sib"]
    rows, width = tok.shape
    group = 4 * rows
    part = width // 4
    collects = core == at["half"]
    first = (h - 2 * at["half"]) * 2 * part + core * 128
    shift = mult(64 * core, 64)
    for p in range(3):
        pltpu.make_async_copy(
            w_qkv.at[:, pl.ds(mult(p * width + first, 128), 256)], wwin.at[p], w_sem.at[p]
        ).start()
    greet(at)

    places = lax.broadcasted_iota(jnp.int32, (8, group), 1)
    begin = jnp.zeros((8, group), jnp.int32)
    edge = lens[0, 0]
    for k in range(1, lens.shape[1] + 1):
        begin = jnp.where(places >= edge, edge, begin)
        if k < lens.shape[1]:
            edge = edge + lens[0, k]
    start_mine[...] = begin.astype(F32)
    st_copy = remote(start_mine, start_sib, st_sem.at[0], st_sem.at[1], (sib, h))
    st_copy.start()

    n, _ = norm_parts(tok[...].astype(F32))
    xn[...] = (n * gain[...] + bias[...]).astype(BF16)

    def shard(ref, s):
        return ref.at[pl.ds(mult(s * rows, rows), rows), :]

    def ag_copy(t):
        return remote(xn, shard(xg, h), ag_send.at[t], ag_recv.at[h], (dp, 2 * core + t))

    for t in range(2):
        @pl.when(2 * core + t != h)
        def _():
            ag_copy(t).start()

    own_fw = remote(xn, shard(xg, h), fw_send.at[0], ag_recv.at[h], (sib, h))

    @pl.when(collects)
    def _():
        own_fw.start()
        xg[pl.ds(mult(h * rows, rows), rows), :] = xn[...]

    for p in range(3):
        pltpu.make_async_copy(wwin.at[p], wwin.at[p], w_sem.at[p]).wait()
        tbuf[...] = wwin[p].T
        wt[p * part : (p + 1) * part, :] = tbuf[pl.ds(shift, part), :]
    wt_copy = pltpu.make_async_copy(wt, wt_o, out_sem.at[0])
    wt_copy.start()
    for p, vec in ((0, bias_q), (2, bias_v)):
        bcol[p] = jnp.broadcast_to(vec[:, pl.ds(mult(first, 128), 256)], (128, 256)).T
    bcol[1] = jnp.zeros((256, 128), F32)

    low = 1 - at["half"]
    order = (h, low * (1 - h) + (1 - low) * (5 - h), 1 + low, 3 * low)

    def fw_copy(d, s):
        return remote(shard(xg, s), shard(xg, s), fw_send.at[d], ag_recv.at[s], (sib, h))

    for d in range(4):
        s = order[d]
        if d == 0:
            @pl.when(jnp.logical_not(collects))
            def _():
                fw_copy(d, s).wait_recv()
        else:
            fw_copy(d, s).wait_recv()

            @pl.when(collects)
            def _():
                fw_copy(d, s).start()

        pltpu.make_async_copy(shard(xg, s), shard(xg_o, s), out_sem.at[1 + d]).start()
        here = xg[pl.ds(mult(s * rows, rows), rows), :]
        for p in range(3):
            res = dot_nt(wt[p * part : (p + 1) * part, :], here) + bcol[p, pl.ds(shift, part), :][:, :1]
            mix[p * part : (p + 1) * part, pl.ds(mult(s * rows, 128), rows)] = res.astype(BF16)
    mix_copy = pltpu.make_async_copy(mix, mix_o, out_sem.at[5])
    mix_copy.start()
    st_copy.wait_recv()
    start_o[...] = jnp.where(collects, start_mine[...], start_sib[...]).astype(jnp.int32)

    heads = part // HEAD_DIM
    scale = SCORE_SCALE * LOG2E

    def at_copy(i, s):
        src = ot.at[pl.ds(mult(i * HEAD_DIM, HEAD_DIM), HEAD_DIM), pl.ds(s * rows, rows)]
        dst = att_o.at[pl.ds(mult(at["block"] * part + i * HEAD_DIM, HEAD_DIM), HEAD_DIM), :]
        return src, dst

    def at_remote(i, s):
        src, dst = at_copy(i, s)
        return remote(src, dst, at_send.at[i * 4 + s], at_recv.at[at["block"] * heads + i], (at["served"], s))

    def stays(s):
        return jnp.logical_and(collects, h == s)

    def one_head(i, _):
        qrow, krow, vrow = (mult(p * part + i * HEAD_DIM, HEAD_DIM) for p in range(3))
        kh[...] = mix[pl.ds(krow, HEAD_DIM), :].T
        for j in range(group // QB):
            cols = slice(j * QB, (j + 1) * QB)
            q_t = mix[pl.ds(qrow, HEAD_DIM), cols]
            begins = start_o[0:1, cols]
            top = jnp.full((1, QB), -jnp.inf, F32)
            for k in range(j + 1):
                s_t = dot(kh[k * QB : (k + 1) * QB, :], q_t)
                key = lax.broadcasted_iota(jnp.int32, (QB, QB), 0)
                keep = key >= begins - k * QB
                if k == j:
                    keep = jnp.logical_and(keep, key <= lax.broadcasted_iota(jnp.int32, (QB, QB), 1))
                s_t = jnp.where(keep, s_t, -1e30)
                scores[k * QB : (k + 1) * QB, :] = s_t
                top = jnp.maximum(top, jnp.max(s_t, axis=0, keepdims=True))
            top = top * scale
            total = jnp.zeros((1, QB), F32)
            acc = jnp.zeros((HEAD_DIM, QB), F32)
            for k in range(j + 1):
                p_t = jnp.exp2(scores[k * QB : (k + 1) * QB, :] * scale - top)
                total = total + jnp.sum(p_t, axis=0, keepdims=True)
                acc = acc + dot(mix[pl.ds(vrow, HEAD_DIM), k * QB : (k + 1) * QB], p_t.astype(BF16))
            ot[pl.ds(qrow, HEAD_DIM), cols] = (acc / total).astype(BF16)
            lse_o[pl.ds(mult(i * 8, 8), 8), cols] = jnp.broadcast_to(top + jnp.log2(total), (8, QB))
        for s in range(4):
            @pl.when(stays(s))
            def _():
                pltpu.make_async_copy(*at_copy(i, s), at_local.at[i]).start()

            @pl.when(jnp.logical_not(stays(s)))
            def _():
                at_remote(i, s).start()
        return 0

    lax.fori_loop(0, heads, one_head, 0)
    ot_copy = pltpu.make_async_copy(ot, ot_o, out_sem.at[6])
    ot_copy.start()

    for t in range(2):
        @pl.when(2 * core + t != h)
        def _():
            ag_copy(t).wait_send()

    @pl.when(collects)
    def _():
        own_fw.wait_send()
        for d in range(1, 4):
            fw_copy(d, order[d]).wait_send()

    st_copy.wait_send()
    wt_copy.wait()
    mix_copy.wait()
    for d in range(4):
        pltpu.make_async_copy(shard(xg, order[d]), shard(xg_o, order[d]), out_sem.at[1 + d]).wait()
    ot_copy.wait()
    for i in range(heads):
        for s in range(4):
            @pl.when(stays(s))
            def _():
                pltpu.make_async_copy(*at_copy(i, s), at_local.at[i]).wait()

            @pl.when(jnp.logical_not(stays(s)))
            def _():
                at_remote(i, s).wait_send()
        for b in range(4):
            dst = att_o.at[pl.ds(b * part + i * HEAD_DIM, HEAD_DIM), :]
            src = ot.at[pl.ds(i * HEAD_DIM, HEAD_DIM), pl.ds(0, rows)]

            @pl.when(jnp.logical_not(jnp.logical_and(collects, at["block"] == b)))
            def _():
                remote(src, dst, at_send.at[i * 4], at_recv.at[b * heads + i], (sib, h)).wait_recv()


def attend(tokens, lengths, gain, bias, bias_q, bias_v, w_qkv):
    rows, width = tokens.shape
    group, part = 4 * rows, width // 4
    heads = part // HEAD_DIM
    dma = pltpu.SemaphoreType.DMA
    return pl.pallas_call(
        attend_kernel,
        out_shape=(
            jax.ShapeDtypeStruct((width, rows), BF16),
            jax.ShapeDtypeStruct((3 * part, group), BF16),
            jax.ShapeDtypeStruct((group, width), BF16),
            jax.ShapeDtypeStruct((part, group), BF16),
            jax.ShapeDtypeStruct((8 * heads, group), F32),
            jax.ShapeDtypeStruct((8, group), jnp.int32),
            jax.ShapeDtypeStruct((3 * part, width), BF16),
        ),
        in_specs=[VMEM, SMEM, VMEM, VMEM, VMEM, VMEM, ANY],
        out_specs=(ANY, ANY, ANY, ANY, VMEM, VMEM, ANY),
        scratch_shapes=[
            pltpu.VMEM((rows, width), BF16),
            pltpu.VMEM((group, width), BF16),
            pltpu.VMEM((3, width, 256), BF16),
            pltpu.VMEM((256, width), BF16),
            pltpu.VMEM((3 * part, width), BF16),
            pltpu.VMEM((3, 256, 128), F32),
            pltpu.VMEM((8, group), F32),
            pltpu.VMEM((8, group), F32),
            pltpu.VMEM((3 * part, group), BF16),
            pltpu.VMEM((group, HEAD_DIM), BF16),
            pltpu.VMEM((group, QB), F32),
            pltpu.VMEM((part, group), BF16),
            dma((3,)), dma((2,)), dma((2,)), dma((4,)), dma((4,)),
            dma((4 * heads,)), dma((4 * heads,)), dma((heads,)), dma((7,)),
        ],
        compiler_params=pltpu.CompilerParams(
            collective_id=0, has_side_effects=True, vmem_limit_bytes=32 << 20
        ),
        name="attend",
    )(tokens, lengths, gain[None], bias[None], bias_q[None], bias_v[None], w_qkv)


def mlp_kernel(
    grad_scale,
    att, tok, cot, b_out, gain, bias, b_fc, b_proj, w_out_h, w_fc_h, w_proj_h,
    out_o, dmid_o, dot_o, gout_o, gfc_o, gproj_o, vec_o,
    w_out, w_fc, w_proj, hid, dfc, dat, gout, gfc, gproj,
    w_sem, send, recv, local, out_sem,
):
    at = place()
    h, core = at["h"], at["core"]
    rows, width = tok.shape
    part = width // 4
    chunks = w_fc_h.shape[1] // width
    wo_copy = pltpu.make_async_copy(w_out_h, w_out, w_sem.at[0])
    wo_copy.start()

    def wf_copy(j):
        return pltpu.make_async_copy(w_fc_h.at[:, pl.ds(j * width, width)], w_fc.at[j], w_sem.at[1 + 2 * j])

    def wp_copy(j):
        return pltpu.make_async_copy(w_proj_h.at[pl.ds(j * width, width), :], w_proj.at[j], w_sem.at[2 + 2 * j])

    for j in range(chunks):
        wf_copy(j).start()
        wp_copy(j).start()
    greet(at)

    dy = cot[...].astype(F32)
    d_proj = (DEPTH_SCALE * dy).astype(BF16)
    wo_copy.wait()
    middle = tok[...].astype(F32) + DEPTH_SCALE * (dot_tn(att[...], w_out[...]) + b_out[...])
    n, r = norm_parts(middle)
    second = (n * gain[...] + bias[...]).astype(BF16)
    result = middle + DEPTH_SCALE * b_proj[...]
    d_second = jnp.zeros((rows, width), F32)
    vec_o[3:4, :] = jnp.sum(dy, axis=0, keepdims=True) * (DEPTH_SCALE * grad_scale)
    for j in range(chunks):
        wf_copy(j).wait()
        u = dot(second, w_fc[j]) + b_fc[j : j + 1, :]
        u2 = u * u
        th = jnp.tanh(GELU_K * u * (1.0 + GELU_A * u2))
        half = 0.5 * (1.0 + th)
        slope = half + 0.5 * u * (1.0 - th * th) * (GELU_K * (1.0 + 3.0 * GELU_A * u2))
        hidden = (u * half).astype(BF16)
        hid[j] = hidden
        wp_copy(j).wait()
        result = result + DEPTH_SCALE * dot(hidden, w_proj[j])
        d_pre = dot_nt(d_proj, w_proj[j]) * slope
        vec_o[4 + j : 5 + j, :] = jnp.sum(d_pre, axis=0, keepdims=True) * grad_scale
        d_fc = d_pre.astype(BF16)
        dfc[j] = d_fc
        d_second = d_second + dot_nt(d_fc, w_fc[j])
    out_o[...] = result
    vec_o[1:2, :] = jnp.sum(d_second * n, axis=0, keepdims=True) * grad_scale
    vec_o[2:3, :] = jnp.sum(d_second, axis=0, keepdims=True) * grad_scale
    d_middle = dy + norm_back(d_second, gain[...], n, r)
    dmid_o[...] = d_middle
    vec_o[0:1, :] = jnp.sum(d_middle, axis=0, keepdims=True) * (DEPTH_SCALE * grad_scale)
    d_out = (DEPTH_SCALE * d_middle).astype(BF16)
    dat[...] = dot_nt(w_out[...], d_out).astype(BF16)

    def target(b):
        return at["even"] + b % 2, 2 * core + b // 2

    def stays(b):
        return jnp.logical_and(core == b % 2, h == 2 * core + b // 2)

    dst = dot_o.at[:, pl.ds(mult(h * rows, 128), rows)]

    def da_local(b):
        return pltpu.make_async_copy(dat.at[pl.ds(b * part, part), :], dst, local)

    def da_remote(b):
        return remote(dat.at[pl.ds(b * part, part), :], dst, send.at[b], recv.at[h], target(b))

    for b in range(4):
        @pl.when(stays(b))
        def _():
            da_local(b).start()

        @pl.when(jnp.logical_not(stays(b)))
        def _():
            da_remote(b).start()

    gout[...] = (dot(att[...], d_out) * grad_scale).astype(BF16)
    go_copy = pltpu.make_async_copy(gout, gout_o, out_sem.at[0])
    go_copy.start()
    second_t = second.T
    gf_copies, gp_copies = [], []
    for j in range(chunks):
        gfc[j] = (dot(second_t, dfc[j]) * grad_scale).astype(BF16)
        gf_copies.append(
            pltpu.make_async_copy(gfc.at[j], gfc_o.at[:, pl.ds(j * width, width)], out_sem.at[1 + 2 * j])
        )
        gf_copies[-1].start()
        gproj[j] = (dot_tn(hid[j], d_proj) * grad_scale).astype(BF16)
        gp_copies.append(
            pltpu.make_async_copy(gproj.at[j], gproj_o.at[pl.ds(j * width, width), :], out_sem.at[2 + 2 * j])
        )
        gp_copies[-1].start()

    served_here = core == at["half"]
    for b in range(4):
        @pl.when(stays(b))
        def _():
            da_local(b).wait()

        @pl.when(jnp.logical_not(stays(b)))
        def _():
            da_remote(b).wait_send()
    for s in range(4):
        @pl.when(jnp.logical_not(jnp.logical_and(served_here, h == s)))
        def _():
            remote(
                dat.at[pl.ds(0, part), :], dot_o.at[:, pl.ds(s * rows, rows)], send.at[0], recv.at[s], (at["sib"], h)
            ).wait_recv()
    go_copy.wait()
    for copy in gf_copies + gp_copies:
        copy.wait()


def mlp(att, tokens, cotangent, grad_scale, b_out, gain, bias, b_fc, b_proj, w_out, w_fc, w_proj):
    rows, width = tokens.shape
    part, group = width // 4, 4 * rows
    ff = w_fc.shape[1]
    chunks = ff // width
    dma = pltpu.SemaphoreType.DMA
    return pl.pallas_call(
        functools.partial(mlp_kernel, grad_scale),
        out_shape=(
            jax.ShapeDtypeStruct((rows, width), F32),
            jax.ShapeDtypeStruct((rows, width), F32),
            jax.ShapeDtypeStruct((part, group), BF16),
            jax.ShapeDtypeStruct((width, width), BF16),
            jax.ShapeDtypeStruct((width, ff), BF16),
            jax.ShapeDtypeStruct((ff, width), BF16),
            jax.ShapeDtypeStruct((8, width), F32),
        ),
        in_specs=[VMEM] * 8 + [ANY] * 3,
        out_specs=(VMEM, VMEM, ANY, ANY, ANY, ANY, VMEM),
        scratch_shapes=[
            pltpu.VMEM((width, width), BF16),
            pltpu.VMEM((chunks, width, width), BF16),
            pltpu.VMEM((chunks, width, width), BF16),
            pltpu.VMEM((chunks, rows, width), BF16),
            pltpu.VMEM((chunks, rows, width), BF16),
            pltpu.VMEM((width, rows), BF16),
            pltpu.VMEM((width, width), BF16),
            pltpu.VMEM((chunks, width, width), BF16),
            pltpu.VMEM((chunks, width, width), BF16),
            dma((1 + 2 * chunks,)), dma((4,)), dma((4,)), dma, dma((1 + 2 * chunks,)),
        ],
        compiler_params=pltpu.CompilerParams(
            collective_id=1, has_side_effects=True, vmem_limit_bytes=56 << 20
        ),
        name="mlp",
    )(
        att, tokens, cotangent, b_out[None], gain[None], bias[None], b_fc.reshape(chunks, width), b_proj[None],
        w_out, w_fc, w_proj,
    )


def back_kernel(
    grad_scale,
    mix_h, xg_h, ot_h, lse, start, do_h, wt_h, dmid, tok, gain,
    gtok_o, gqkv_o, ln_o, bias_o,
    mix, xg, ot, do_t, wt, delta, kh, vh, qh, doh, dq, dk, dv, dmix, partial, summed, arrive, arrive2, gq,
    in_sem, sw_send, sw_recv, fin_send, fin_recv, fin_local, out_sem,
):
    at = place()
    h, core, sib = at["h"], at["core"], at["sib"]
    rows, width = tok.shape
    part, group = width // 4, 4 * rows
    heads = part // HEAD_DIM
    loads = [
        pltpu.make_async_copy(src, dst, in_sem.at[k])
        for k, (src, dst) in enumerate(((do_h, do_t), (ot_h, ot), (mix_h, mix), (wt_h, wt), (xg_h, xg)))
    ]
    for load in loads:
        load.start()
    greet(at)
    for load in loads[:3]:
        load.wait()
    scale = SCORE_SCALE * LOG2E

    def one_head(i, _):
        qrow, krow, vrow = (mult(p * part + i * HEAD_DIM, HEAD_DIM) for p in range(3))
        d_head = do_t[pl.ds(qrow, HEAD_DIM), :]
        delta[...] = jnp.broadcast_to(
            jnp.sum(d_head.astype(F32) * ot[pl.ds(qrow, HEAD_DIM), :].astype(F32), axis=0, keepdims=True), (8, group)
        )
        qh[...] = mix[pl.ds(qrow, HEAD_DIM), :].T
        kh[...] = mix[pl.ds(krow, HEAD_DIM), :].T
        vh[...] = mix[pl.ds(vrow, HEAD_DIM), :].T
        doh[...] = d_head.T
        for j in range(group // QB):
            cols = slice(j * QB, (j + 1) * QB)
            q_t = mix[pl.ds(qrow, HEAD_DIM), cols]
            do_j = do_t[pl.ds(qrow, HEAD_DIM), cols]
            begins = start[0:1, cols]
            lse_j = lse[pl.ds(mult(i * 8, 8), 8), cols][0:1]
            delta_j = delta[0:1, cols]
            acc = jnp.zeros((HEAD_DIM, QB), F32)
            for k in range(j + 1):
                keys = slice(k * QB, (k + 1) * QB)
                s_t = dot(kh[keys, :], q_t)
                key = lax.broadcasted_iota(jnp.int32, (QB, QB), 0)
                keep = key >= begins - k * QB
                if k == j:
                    keep = jnp.logical_and(keep, key <= lax.broadcasted_iota(jnp.int32, (QB, QB), 1))
                p_t = jnp.where(keep, jnp.exp2(s_t * scale - lse_j), 0.0)
                dp_t = dot(vh[keys, :], do_j)
                ds_t = (p_t * (dp_t - delta_j)).astype(BF16)
                dv_add = dot(p_t.astype(BF16), doh[cols, :])
                dk_add = dot(ds_t, qh[cols, :])
                if k == j:
                    dv[keys, :] = dv_add
                    dk[keys, :] = dk_add
                else:
                    dv[keys, :] += dv_add
                    dk[keys, :] += dk_add
                acc = acc + dot(mix[pl.ds(krow, HEAD_DIM), keys], ds_t)
            dmix[pl.ds(qrow, HEAD_DIM), cols] = (acc * SCORE_SCALE).astype(BF16)
        dmix[pl.ds(krow, HEAD_DIM), :] = (dk[...] * SCORE_SCALE).T.astype(BF16)
        dmix[pl.ds(vrow, HEAD_DIM), :] = dv[...].T.astype(BF16)
        return 0

    lax.fori_loop(0, heads, one_head, 0)
    loads[3].wait()
    loads[4].wait()

    def rows_of(s):
        return pl.ds(mult(s * rows, rows), rows)

    def part_of(s):
        return dot_tn(dmix[:, pl.ds(mult(s * rows, 128), rows)], wt[...])

    swaps = []
    for t in range(2):
        partial[t] = part_of(2 * t + 1 - core).astype(BF16)
        swaps.append(remote(partial.at[t], arrive.at[t], sw_send.at[t], sw_recv.at[t], (sib, h)))
        swaps[-1].start()

    slot = h - 2 * at["half"]

    def fin_remote(t):
        return remote(
            summed.at[t], arrive2.at[slot], fin_send.at[t], fin_recv.at[slot], (at["served"], 2 * t + core)
        )

    def fin_local_copy(t):
        return pltpu.make_async_copy(summed.at[t], arrive2.at[slot], fin_local)

    def stays(t):
        return jnp.logical_and(core == at["half"], h == 2 * t + core)

    for t in range(2):
        mine = part_of(2 * t + core)
        swaps[t].wait_recv()
        summed[t] = (mine + arrive[t].astype(F32)).astype(BF16)

        @pl.when(stays(t))
        def _():
            fin_local_copy(t).start()

        @pl.when(jnp.logical_not(stays(t)))
        def _():
            fin_remote(t).start()

    ones = jnp.ones((group, 128), BF16)
    bias_o[...] = dot(dmix[...], ones) * grad_scale
    gq[...] = (dot(dmix[...], xg[...]) * grad_scale).astype(BF16)
    gq_copy = pltpu.make_async_copy(gq, gqkv_o, out_sem)
    gq_copy.start()

    for k in range(2):
        from_me = jnp.logical_and(
            jnp.logical_and(core == at["half"], slot == k), lax.rem(h, 2) == core
        )

        @pl.when(from_me)
        def _():
            pltpu.make_async_copy(summed.at[0], arrive2.at[k], fin_local).wait()

        @pl.when(jnp.logical_not(from_me))
        def _():
            remote(summed.at[0], arrive2.at[k], fin_send.at[0], fin_recv.at[k], (sib, h)).wait_recv()
    e = arrive2[0].astype(F32) + arrive2[1].astype(F32)
    n, r = norm_parts(tok[...].astype(F32))
    gtok_o[...] = dmid[...] + norm_back(e, gain[...], n, r)
    ln_o[0:1, :] = jnp.sum(e * n, axis=0, keepdims=True) * grad_scale
    ln_o[1:2, :] = jnp.sum(e, axis=0, keepdims=True) * grad_scale
    ln_o[2:8, :] = jnp.zeros((6, width), F32)
    for t in range(2):
        swaps[t].wait_send()

        @pl.when(jnp.logical_not(stays(t)))
        def _():
            fin_remote(t).wait_send()
    gq_copy.wait()


def attend_back(mix, xg, ot, lse, start, d_ot, wt, d_middle, tokens, gain, grad_scale):
    rows, width = tokens.shape
    part, group = width // 4, 4 * rows
    dma = pltpu.SemaphoreType.DMA
    return pl.pallas_call(
        functools.partial(back_kernel, grad_scale),
        out_shape=(
            jax.ShapeDtypeStruct((rows, width), F32),
            jax.ShapeDtypeStruct((3 * part, width), BF16),
            jax.ShapeDtypeStruct((8, width), F32),
            jax.ShapeDtypeStruct((3 * part, 128), F32),
        ),
        in_specs=[ANY, ANY, ANY, VMEM, VMEM, ANY, ANY, VMEM, VMEM, VMEM],
        out_specs=(VMEM, ANY, VMEM, VMEM),
        scratch_shapes=[
            pltpu.VMEM((3 * part, group), BF16),
            pltpu.VMEM((group, width), BF16),
            pltpu.VMEM((part, group), BF16),
            pltpu.VMEM((part, group), BF16),
            pltpu.VMEM((3 * part, width), BF16),
            pltpu.VMEM((8, group), F32),
            pltpu.VMEM((group, HEAD_DIM), BF16),
            pltpu.VMEM((group, HEAD_DIM), BF16),
            pltpu.VMEM((group, HEAD_DIM), BF16),
            pltpu.VMEM((group, HEAD_DIM), BF16),
            pltpu.VMEM((HEAD_DIM, group), F32),
            pltpu.VMEM((group, HEAD_DIM), F32),
            pltpu.VMEM((group, HEAD_DIM), F32),
            pltpu.VMEM((3 * part, group), BF16),
            pltpu.VMEM((2, rows, width), BF16),
            pltpu.VMEM((2, rows, width), BF16),
            pltpu.VMEM((2, rows, width), BF16),
            pltpu.VMEM((2, rows, width), BF16),
            pltpu.VMEM((3 * part, width), BF16),
            dma((5,)), dma((2,)), dma((2,)), dma((2,)), dma((2,)), dma, dma,
        ],
        compiler_params=pltpu.CompilerParams(
            collective_id=2, has_side_effects=True, vmem_limit_bytes=48 << 20
        ),
        name="attend_back",
    )(mix, xg, ot, lse, start, d_ot, wt, d_middle, tokens, gain[None])


def shards(
    tokens, lengths, ln1_gain, ln1_bias, w_qkv, bias_q, bias_v, w_out, bias_out, ln2_gain, ln2_bias, w_fc, bias_fc,
    w_proj, bias_proj, cotangent,
):
    rows, width = tokens.shape
    part = width // 4
    device_count = lax.axis_size("dp") * lax.axis_size("head")
    grad_scale = 1.0 / math.sqrt(rows * device_count)
    att, mix, xg, ot, lse, start, wt = attend(tokens, lengths, ln1_gain, ln1_bias, bias_q, bias_v, w_qkv)
    block_output, d_middle, d_ot, g_out, g_fc, g_proj, vecs = mlp(
        att, tokens, cotangent, grad_scale, bias_out, ln2_gain, ln2_bias, bias_fc, bias_proj, w_out, w_fc, w_proj
    )
    grad_tokens, g_qkv, ln_vec, bias_vec = attend_back(
        mix, xg, ot, lse, start, d_ot, wt, d_middle, tokens, ln1_gain, grad_scale
    )
    block = lax.rem(lax.axis_index("head"), 2) * 2 + lax.rem(lax.axis_index("dp"), 2)
    wide = jnp.zeros((3, width, width), BF16)
    wide = lax.dynamic_update_slice(wide, g_qkv.reshape(3, part, width), (0, block * part, 0))
    wide = wide.reshape(3 * width, width).T
    bias_wide = lax.dynamic_update_slice(
        jnp.zeros((3, width), F32), bias_vec[:, 0].reshape(3, part), (0, block * part)
    )

    def reduce_mat(g, dim):
        share = lax.psum_scatter(g, "dp", scatter_dimension=dim, tiled=True)
        return lax.psum(share, "head").astype(F32)

    vec = lax.psum(jnp.concatenate([vecs, ln_vec[:2], bias_wide]), ("dp", "head"))
    return (
        block_output, grad_tokens, vec[8], vec[9], reduce_mat(wide, 0), vec[10], vec[12], reduce_mat(g_out, 0),
        vec[0], vec[1], vec[2], reduce_mat(g_fc, 1), vec[4:8].reshape(-1), reduce_mat(g_proj, 0), vec[3],
    )


def solution(mesh):
    rows = P(("dp", "head"), None)
    return jax.shard_map(
        shards,
        mesh=mesh,
        in_specs=(rows, P("dp", None)) + (P(),) * 13 + (rows,),
        out_specs=(
            rows, rows, P(), P(), P("dp", None), P(), P(), P("dp", None), P(), P(), P(), P(None, "dp"), P(),
            P("dp", None), P(),
        ),
        check_vma=False,
    )
```

time: 753 us -> 478 us (0.63)
  matrix products: 276 us -> 0 us
  waiting for transfers between devices: 120 us -> 248 us
  Pallas kernels: 0 us -> 125 us
  other arithmetic: 116 us -> 4.9 us
  blocking collectives: 137 us -> 42.3 us
  local copies, waits for them, and re-layouts: 67.3 us -> 42.2 us
  starting transfers between devices: 10.9 us -> 0.2 us
    dot_general x33 -> x0, matrix products: 276 us -> none  [the longest x3 66 us: one_block(): jnp.einsum('hqk,qhd->khd', score_grad, query_block, preferred_element_typ...]
    pallas_call x0 -> x3, Pallas kernels: none -> 125 us  [the longest x1 52.8 us: attend(): pl.pallas_call(attend_kernel, out_shape=(jax.ShapeDtypeStruct((width, row...]
    unnamed x6 -> x7, waiting for transfers between devices: 0.08 us -> 110 us
    all_to_all x2 -> x0, blocking collectives: 93.8 us -> none  [the longest x1 75.6 us: shards(): lax.all_to_all(group_mixed_grad, 'head', split_axis=0, concat_axis=2, til...]
    sub x6 -> x0, other arithmetic: 87.8 us -> none  [block_weights(): weights = jnp.exp(scores - largest)]
    reduce_scatter x3 -> x2, waiting for transfers between devices: 31.4 us -> 95.5 us  [reduce_mat(): share = lax.psum_scatter(g, 'dp', scatter_dimension=dim, tiled=True)]
    all_to_all x2 -> x0, waiting for transfers between devices: 60.2 us -> none  [the longest x1 53.5 us: forward(): lax.all_to_all(mixed_rows.reshape(tok_rows, 3, model_width), 'head', spli...]
    unnamed x94 -> x31, local copies, waits for them, and re-layouts: 12.9 us -> 31 us
  transfers between devices with their start and end apart: 7 -> 5, of which waited for: 4 -> 5; matrix products, arithmetic and copies ran while one was open for 41% -> 3% of each run, Pallas kernels for 0% -> 0%
where the time goes in v2:
time: 478 us; the launch traced here: 477 us
  waiting for transfers between devices  248 us (52%)
  Pallas kernels  125 us (26%)
  blocking collectives  42.3 us (9%)
  local copies, waits for them, and re-layouts  42.2 us (9%)
  between operations  13.9 us (3%)
  other arithmetic  4.9 us (1%)
    unnamed x7, waiting for transfers between devices  110 us
    reduce_scatter x2, waiting for transfers between devices, reduce_mat(): share = lax.psum_scatter(g, 'dp', scatter_dimension=dim, tiled=True)  95.5 us
    pallas_call x1, Pallas kernels, attend(): pl.pallas_call(attend_kernel, out_shape=(jax.ShapeDtypeStruct((width, row...  52.8 us
    psum x1, waiting for transfers between devices, reduce_mat(): return lax.psum(share, 'head').astype(F32)  42.4 us
    pallas_call x1, Pallas kernels, attend_back(): pl.pallas_call(functools.partial(back_kernel, grad_scale), out_shape=(jax...  42.4 us
    psum x1, blocking collectives, shards(): lax.psum(jnp.concatenate([vecs, ln_vec[:2], bias_wide]), ('dp', 'head'))  42.3 us
    unnamed x31, local copies, waits for them, and re-layouts  31 us
    pallas_call x1, Pallas kernels, mlp(): pl.pallas_call(functools.partial(mlp_kernel, grad_scale), out_shape=(jax....  29.9 us
  transfers between devices with their start and end apart: 5, of which 5 were waited for; matrix products, arithmetic and copies ran while one was open for 3% of the time, Pallas kernels for 0%

profile of v2, /device:TPU:0, one launch (start us, length us, event | category | flops | bytes accessed | tf_op | source)
XLA Modules:
  0.0 476.9 jit_solution(15671002359387966378)
XLA Ops:
  7.2 0.7 broadcast_in_dim.31.gain
  10.0 1.3 broadcast_in_dim.35.b_out
  11.3 1.3 broadcast_in_dim.36.gain
  12.5 1.3 broadcast_in_dim.37.bias
  13.8 1.3 reshape.42.b_fc
  15.1 1.3 broadcast_in_dim.38.b_proj
  16.4 1.1 copy-done
  17.4 2.0 copy-done.2
  20.1 52.8 %attend.1 = (bf16[768,384]{1,0:T(8,128)(2,1)S(1)}, bf16[576,1536]{1,0:T(8,128)(2,1)S(1)}, bf16[1536,768]{1,0:T(8,128)(2,1)S(1)}, bf16[192,1536]{1,0:T(8,128)(2,1...) custom-call(bf16[384,768]{1,0:T(8,128)(2,1)S(1)} %copy-done, ...), custom_call_target="tpu_custom_call" | custom-call | tf_op jit(solution)/shard_map/attend/pallas_call | solution.py:276
  72.9 1.4 copy-done.3
  74.3 1.3 copy-done.4
  75.6 0.8 copy-done.6
  76.4 29.9 %mlp.1 = (f32[384,768]{1,0:T(8,128)}, f32[384,768]{1,0:T(8,128)}, bf16[192,1536]{1,0:T(8,128)(2,1)}, bf16[768,768]{1,0:T(8,128)(2,1)}, bf16[768,3072]{1,0:T(8,12...) custom-call(bf16[768,384]{1,0:T(8,128)(2,1)} %copy-done.6, bf16[384,768]{1,0:T(8,128)(2,1)} %tok.5, ...), custom_call_target="tpu_custom_call" | custom-call | tf_op jit(solution)/shard_map/mlp/pallas_call | solution.py:438
  106.4 1.1 copy-done.5
  107.5 42.4 %attend_back.1 = (f32[384,768]{1,0:T(8,128)S(1)}, bf16[576,768]{1,0:T(8,128)(2,1)S(1)}, f32[8,768]{1,0:T(8,128)S(1)}, f32[576,128]{1,0:T(8,128)S(1)}) custom-call(bf16[576,1536]{1,0:T(8,128)(2,1)} %copy-done.4, bf16[1536,768]{1,0:T(8,128)(2,1)} %copy-done.3, bf16[192,1536]{1,0:T(8,128)(2,1)S(1)} %get-tuple-element.37.ot_h, ...), custom_call_target="tpu_custom_call" | custom-call | tf_op jit(solution)/shard_map/attend_back/pallas_call | solution.py:617
  150.2 1.8 copy-done.8
  151.9 5.8 %copy.34 = bf16[768,2304]{1,0:T(8,128)(2,1)} copy(bf16[768,2304]{0,1:T(8,128)(2,1)} %bitcast.9) | data formatting | bytes 7077888
  157.8 6.6 %copy.36 = bf16[768,3072]{0,1:T(8,128)(2,1)} copy(bf16[768,3072]{1,0:T(8,128)(2,1)} %get-tuple-element.49) | data formatting | bytes 9437184
  165.8 53.8 %reduce-scatter.13.cloned.1.call-done = bf16[96,2304]{1,0:T(8,128)(2,1)} async-done(((bf16[768,2304]{1,0:T(8,128)(2,1)}), bf16[96,2304]{1,0:T(8,128)(2,1)}) %reduce-scatter.13.cloned.1.call-update) | async-done | bytes 442384
  219.6 2.1 copy.35
  221.7 55.3 %reduce-scatter.15.cloned.1.call-done = bf16[384,768]{1,0:T(8,128)(2,1)} async-done(((bf16[3072,768]{1,0:T(8,128)(2,1)}), bf16[384,768]{1,0:T(8,128)(2,1)}) %reduce-scatter.15.cloned.1.call-update) | async-done | bytes 589840
  277.0 2.1 copy.37
  279.1 38.3 %reduce-scatter.9.cloned.1.call-done = bf16[96,768]{1,0:T(8,128)(2,1)} async-done(((bf16[768,768]{1,0:T(8,128)(2,1)}), bf16[96,768]{1,0:T(8,128)(2,1)}) %reduce-scatter.9.cloned.1.call-update) | async-done | bytes 147472 | tf_op jit(solution)/shard_map/reduce_scatter | solution.py:680
  317.3 57.2 %reduce-scatter.11.cloned.1.call-done = bf16[384,768]{1,0:T(8,128)(2,1)} async-done(((bf16[3072,768]{1,0:T(8,128)(2,1)}), bf16[384,768]{1,0:T(8,128)(2,1)}) %reduce-scatter.11.cloned.1.call-update) | async-done | bytes 589840 | tf_op jit(solution)/shard_map/reduce_scatter | solution.py:680
  375.1 42.3 %psum.35 = f32[13,768]{1,0:T(8,128)S(1)} all-reduce(f32[13,768]{1,0:T(8,128)S(1)} %pad_maximum_fusion), channel_id=1, replica_groups=mesh['dp'=8,'head'=4] {'dp','head'}, use_global_device_ids=true, to_apply=%region_0.0 | all-reduce | flops 9984 | bytes 79872 | tf_op jit(solution)/shard_map/psum | solution.py:683
  418.7 42.4 %all-reduce.3.cloned.1.call-done = (bf16[96,2304]{0,1:T(8,128)(2,1)}, bf16[96,768]{1,0:T(8,128)(2,1)}, bf16[768,384]{1,0:T(8,128)(2,1)}, bf16[384,768]{1,0:T(8,128)(2,1)}) async-done(((bf16[96,2304]{0,1:T(8,128)(2,1)}, bf16[96,768]{1,0:T(8,128)(2,1)}, bf16[768,384]{1,0:T(8,128)(2,1)}, bf16[384,768]{1,0:T(8,128)(2,1)}), (bf16[96,2304]{0,1:T(8,128)(2,1)}, bf16[96,768]{1,0:T(8,128)(2,1)}, ...) | async-done | bytes 1769488 | tf_op jit(solution)/shard_map/psum | solution.py:681
  461.2 2.3 copy.33
  463.4 1.6 convert_element_type.13
  465.1 2.2 convert_element_type.14
  467.2 1.1 convert_element_type.15
  468.3 1.0 copy.46
  469.3 1.0 copy.47
  (41 shorter events, 6.3 us)
Async XLA Ops:
  7.2 212.4 %reduce-scatter.13.cloned.1.call-start = ((), (), s32[]{:S(2)}) async-start(), calls=%async_computation.6 | async-start | bytes 3981312
  16.4 1.1 copy-start
  17.4 2.0 copy-start.2
  19.4 0.7 copy-start.7
  72.9 1.4 copy-start.3
  74.3 1.3 copy-start.4
  75.6 0.8 copy-start.6
  76.4 29.9 %copy-start.1 = (bf16[384,768]{1,0:T(8,128)(2,1)S(1)}, bf16[384,768]{1,0:T(8,128)(2,1)}, u32[]{:S(2)}) copy-start(bf16[384,768]{1,0:T(8,128)(2,1)} %tok.5) | copy-start | bytes 1769476
  106.4 1.1 copy-start.5
  150.2 1.8 copy-start.8
  157.8 119.2 %reduce-scatter.15.cloned.1.call-start = ((), (), s32[]{:S(2)}) async-start(), calls=%async_computation.7 | async-start | bytes 5308416
  164.5 152.9 %reduce-scatter.9.cloned.1.call-start = ((), (), s32[]{:S(2)}) async-start(), calls=%async_computation.4 | async-start | bytes 1327104 | tf_op jit(solution)/shard_map/reduce_scatter | solution.py:680
  165.2 209.3 %reduce-scatter.11.cloned.1.call-start = ((), (), s32[]{:S(2)}) async-start(), calls=%async_computation.5 | async-start | bytes 5308416 | tf_op jit(solution)/shard_map/reduce_scatter | solution.py:680
  165.3 209.8 %copy-start.11 = (f32[8,768]{1,0:T(8,128)S(1)}, f32[8,768]{1,0:T(8,128)}, u32[]{:S(2)}) copy-start(f32[8,768]{1,0:T(8,128)} %get-tuple-element.44) | copy-start | bytes 73732
  165.8 295.4 %all-reduce.3.cloned.1.call-start = ((), (), s32[]{:S(2)}) async-start(), calls=%async_computation.8 | async-start | bytes 3833856 | tf_op jit(solution)/shard_map/psum | solution.py:681
  374.6 93.8 %copy-start.9 = (f32[384,768]{1,0:T(8,128)S(1)}, f32[384,768]{1,0:T(8,128)}, u32[]{:S(2)}) copy-start(f32[384,768]{1,0:T(8,128)} %get-tuple-element.108) | copy-start | bytes 3538948
  461.2 6.1 %copy-start.10 = (bf16[384,768]{1,0:T(8,128)(2,1)S(1)}, bf16[384,768]{1,0:T(8,128)(2,1)}, u32[]{:S(2)}) copy-start(bf16[384,768]{1,0:T(8,128)(2,1)} %get-tuple-element.92) | copy-start | bytes 1769476
Sparse Core Ops, SparseCore 0:
  157.9 61.6 reduce-scatter.12
  223.0 53.8 reduce-scatter.14
  280.5 36.7 reduce-scatter.8
  320.6 53.8 reduce-scatter.10
  378.4 82.7 all-reduce.2
